TPU v7x, 32 devices: a whole 2x2x4 slice. The times are simulated.
32 devices in a mesh: shard: 2 (over x), ctx: 4 (over y, core), tp: 4 (over z).
Axes of the slice: x: 2, y: 2, z: 4, core: 2. Of those that a mesh axis runs over, the one named last changes fastest.
Arguments:
- tokens: bfloat16 [2, 16, 196, 768], P('shard', 'ctx', 'tp'), may hold values from -6 to 6
- cotangent: bfloat16 [2, 16, 196, 768], P('shard', 'ctx', 'tp'), may hold values from -6 to 6
- norm_gains: bfloat16 [3, 768], P(None, 'shard'), may hold values from 0.099609375 to 1.8984375
- norm_shifts: bfloat16 [3, 768], P(None, 'shard'), may hold values from -1.5 to 1.5
- qkv_spatial: bfloat16 [3, 768, 768], P(None, 'shard', 'tp'), may hold values from -0.21875 to 0.21875
- proj_spatial: bfloat16 [768, 768], P('tp', 'shard'), may hold values from -0.75 to 0.75
- qkv_temporal: bfloat16 [3, 768, 768], P(None, 'shard', 'tp'), may hold values from -0.21875 to 0.21875
- proj_temporal: bfloat16 [768, 768], P('tp', 'shard'), may hold values from -0.4375 to 0.4375
- up_weight: bfloat16 [768, 3072], P('shard', 'tp'), may hold values from -0.21875 to 0.21875
- down_weight: bfloat16 [3072, 768], P('tp', 'shard'), may hold values from -0.109375 to 0.109375
- out_bias: bfloat16 [3, 768], P(None, 'shard'), may hold values from -1.5 to 1.5
- qv_bias: bfloat16 [2, 2, 768], P(None, None, 'shard'), may hold values from -1.5 to 1.5
- up_bias: bfloat16 [3072], P('shard'), may hold values from -1.5 to 1.5
Outputs:
- activations: bfloat16 [2, 16, 196, 768], P('shard', 'ctx', 'tp')
- token_grad: float32 [2, 16, 196, 768], P('shard', 'ctx', 'tp')
- norm_gains_grad: float32 [3, 768], P(None, ('shard', 'ctx', 'tp'))
- norm_shifts_grad: float32 [3, 768], P(None, ('shard', 'ctx', 'tp'))
- qkv_spatial_grad: float32 [3, 768, 768], P(None, ('shard', 'ctx'), 'tp')
- proj_spatial_grad: float32 [768, 768], P('tp', ('shard', 'ctx'))
- qkv_temporal_grad: float32 [3, 768, 768], P(None, ('shard', 'ctx'), 'tp')
- proj_temporal_grad: float32 [768, 768], P('tp', ('shard', 'ctx'))
- up_weight_grad: float32 [768, 3072], P(('shard', 'ctx'), 'tp')
- down_weight_grad: float32 [3072, 768], P('tp', ('shard', 'ctx'))
- out_bias_grad: float32 [3, 768], P(None, ('shard', 'ctx', 'tp'))
- qv_bias_grad: float32 [2, 2, 768], P(None, None, ('shard', 'ctx', 'tp'))
- up_bias_grad: float32 [3072], P(('shard', 'ctx', 'tp'))
All inputs are finite; a program needn't handle non-finite values.
Results may differ from a plain program's by a relative error of at most 0.023.
Values may be sent and summed in bfloat16 or wider, within the bound.
No kernel may reach another device: no remote copies, remote signals or barrier semaphores. Data moves between devices by JAX's collectives and lax.ppermute only.
A program may use at most 128 MiB of HBM per device.

v0:
```python
import jax
import jax.numpy as jnp
from jax import lax
from jax.sharding import PartitionSpec as P

HD = 64


norm_eps = 1e-06
space_forms = ("bqhd,bkhd->bhqk", "bhqk,bkhd->bqhd", "bhqk,bqhd->bkhd")
time_forms = ("cqphd,ckphd->cphqk", "cphqk,ckphd->cqphd", "cphqk,cqphd->ckphd")


def normalize(features, gain_row, shift_row):
    average = jnp.mean(features, axis=-1, keepdims=True)
    centered = features - average
    variance = jnp.mean(centered * centered, axis=-1, keepdims=True)
    return centered * lax.rsqrt(variance + norm_eps) * gain_row + shift_row


def activate(features):
    return jax.nn.gelu(features, approximate=False)


def matmul(left_term, right_term):
    return jnp.dot(left_term, right_term, preferred_element_type=jnp.float32)


def heads_in(normed_flat, weight_triple, bias_pair):
    projected = jnp.einsum(
        "rd,tde->tre", normed_flat, weight_triple, preferred_element_type=jnp.float32
    )
    biases = jnp.stack([bias_pair[0], jnp.zeros_like(bias_pair[0]), bias_pair[1]])
    return (projected + biases[:, None, :]).astype(jnp.bfloat16)


def weight_side(normed_flat, grad_triple, weight_triple):
    grad_weights = jnp.einsum(
        "rd,tre->tde", normed_flat, grad_triple, preferred_element_type=jnp.float32
    )
    column_sums = jnp.sum(grad_triple, axis=1, dtype=jnp.float32)
    grad_normed = jnp.einsum(
        "tre,tde->rd", grad_triple, weight_triple, preferred_element_type=jnp.float32
    )
    return (grad_weights, jnp.stack([column_sums[0], column_sums[2]]), grad_normed)


def attend(queries, key_rows, values, form_triple):
    score_form, out_form, key_form = form_triple
    scores = jnp.einsum(score_form, queries, key_rows, preferred_element_type=jnp.float32) * HD ** (
        -0.5
    )
    row_max = jnp.max(scores, axis=-1, keepdims=True)
    shifted = jnp.exp(scores - row_max)
    row_total = jnp.sum(shifted, axis=-1, keepdims=True)
    weights = (shifted / row_total).astype(jnp.bfloat16)
    attended = jnp.einsum(out_form, weights, values, preferred_element_type=jnp.float32)
    return (attended, row_max + jnp.log(row_total))


def attend_back(queries, key_rows, values, log_total, grad_out, form_triple):
    score_form, out_form, key_form = form_triple
    scores = jnp.einsum(score_form, queries, key_rows, preferred_element_type=jnp.float32) * HD ** (
        -0.5
    )
    weights = jnp.exp(scores - log_total)
    grad_values = jnp.einsum(
        key_form, weights.astype(jnp.bfloat16), grad_out, preferred_element_type=jnp.float32
    )
    grad_weights = jnp.einsum(score_form, grad_out, values, preferred_element_type=jnp.float32)
    inner = jnp.sum(grad_weights * weights, axis=-1, keepdims=True)
    grad_scores = (weights * (grad_weights - inner)).astype(jnp.bfloat16)
    grad_queries = jnp.einsum(
        out_form, grad_scores, key_rows, preferred_element_type=jnp.float32
    ) * HD ** (-0.5)
    grad_keys = jnp.einsum(
        key_form, grad_scores, queries, preferred_element_type=jnp.float32
    ) * HD ** (-0.5)
    return (grad_queries, grad_keys, grad_values)


def spread_rows(normed_share):
    return lax.all_gather(normed_share, "tp", axis=2, tiled=True)


def collect_rows(partial_full):
    return lax.psum_scatter(
        partial_full.astype(jnp.bfloat16), "tp", scatter_dimension=2, tiled=True
    ).astype(jnp.float32)


def spread_grads(grad_share):
    return lax.all_gather(grad_share, "tp", axis=2, tiled=True)


def collect_grads(partial_full):
    return lax.psum_scatter(
        partial_full.astype(jnp.bfloat16), "tp", scatter_dimension=2, tiled=True
    ).astype(jnp.float32)


def unpack(gathered, tp_rank, head_cols, hidden_cols):
    (
        gain_rows,
        shift_rows,
        space_qkv,
        space_proj,
        time_qkv,
        time_proj,
        up_gathered,
        down_gathered,
        bias_rows,
        qv_whole,
        up_whole,
    ) = gathered
    qv_here = lax.dynamic_slice_in_dim(qv_whole, tp_rank * head_cols, head_cols, 2).astype(
        jnp.float32
    )
    up_here = lax.dynamic_slice_in_dim(up_whole, tp_rank * hidden_cols, hidden_cols, 0).astype(
        jnp.float32
    )
    return (
        gain_rows.astype(jnp.float32),
        shift_rows.astype(jnp.float32),
        space_qkv,
        space_proj,
        time_qkv,
        time_proj,
        up_gathered,
        down_gathered,
        bias_rows.astype(jnp.float32),
        qv_here,
        up_here,
    )


def on_device(
    tokens,
    cotangent,
    norm_gains,
    norm_shifts,
    qkv_spatial,
    proj_spatial,
    qkv_temporal,
    proj_temporal,
    up_weight,
    down_weight,
    out_bias,
    qv_bias,
    up_bias,
):
    tp_rank = lax.axis_index("tp")
    tp_count = lax.axis_size("tp")
    clip_count, frames, patch_share, model_width = tokens.shape
    patches = patch_share * tp_count
    head_cols = qkv_spatial.shape[2]
    head_count = head_cols // HD
    hidden_cols = up_weight.shape[1]
    row_count = clip_count * frames * patches
    full_shape = (clip_count, frames, patches, model_width)
    space_shape = (clip_count * frames, patches, head_count, HD)
    time_shape = (clip_count, frames, patches, head_count, HD)
    gathered = (
        lax.all_gather(norm_gains, "shard", axis=1, tiled=True),
        lax.all_gather(norm_shifts, "shard", axis=1, tiled=True),
        lax.all_gather(qkv_spatial, "shard", axis=1, tiled=True),
        lax.all_gather(proj_spatial, "shard", axis=1, tiled=True),
        lax.all_gather(qkv_temporal, "shard", axis=1, tiled=True),
        lax.all_gather(proj_temporal, "shard", axis=1, tiled=True),
        lax.all_gather(up_weight, "shard", axis=0, tiled=True),
        lax.all_gather(down_weight, "shard", axis=1, tiled=True),
        lax.all_gather(out_bias, "shard", axis=1, tiled=True),
        lax.all_gather(qv_bias, "shard", axis=2, tiled=True),
        lax.all_gather(up_bias, "shard", axis=0, tiled=True),
    )
    (
        gain_rows,
        shift_rows,
        space_qkv,
        space_proj,
        time_qkv,
        time_proj,
        up_gathered,
        down_gathered,
        bias_rows,
        qv_here,
        up_here,
    ) = unpack(gathered, tp_rank, head_cols, hidden_cols)
    residual_in = tokens.astype(jnp.float32)
    space_normed = spread_rows(
        normalize(residual_in, gain_rows[0], shift_rows[0]).astype(jnp.bfloat16)
    )
    space_normed = space_normed.reshape(row_count, model_width)
    space_triple = heads_in(space_normed, space_qkv, qv_here[0])
    space_query = space_triple[0].reshape(space_shape)
    space_keys = space_triple[1].reshape(space_shape)
    space_values = space_triple[2].reshape(space_shape)
    space_out, space_total = attend(space_query, space_keys, space_values, space_forms)
    space_out = space_out.reshape(row_count, head_cols).astype(jnp.bfloat16)
    after_space = (
        residual_in + collect_rows(matmul(space_out, space_proj).reshape(full_shape)) + bias_rows[0]
    )
    time_normed = spread_rows(
        normalize(after_space, gain_rows[1], shift_rows[1]).astype(jnp.bfloat16)
    )
    time_normed = time_normed.reshape(row_count, model_width)
    time_triple = heads_in(time_normed, time_qkv, qv_here[1])
    time_query = time_triple[0].reshape(time_shape)
    time_keys, time_values = (
        lax.all_gather(time_triple[1].reshape(time_shape), "ctx", axis=1, tiled=True),
        lax.all_gather(time_triple[2].reshape(time_shape), "ctx", axis=1, tiled=True),
    )
    time_out, time_total = attend(time_query, time_keys, time_values, time_forms)
    time_out = time_out.reshape(row_count, head_cols).astype(jnp.bfloat16)
    after_time = (
        after_space + collect_rows(matmul(time_out, time_proj).reshape(full_shape)) + bias_rows[1]
    )
    mlp_normed = spread_rows(
        normalize(after_time, gain_rows[2], shift_rows[2]).astype(jnp.bfloat16)
    )
    mlp_normed = mlp_normed.reshape(row_count, model_width)
    hidden_pre = matmul(mlp_normed, up_gathered) + up_here
    hidden_act = activate(hidden_pre).astype(jnp.bfloat16)
    finished = (
        after_time
        + collect_rows(matmul(hidden_act, down_gathered).reshape(full_shape))
        + bias_rows[2]
    )
    gathered = (
        lax.all_gather(norm_gains, "shard", axis=1, tiled=True),
        lax.all_gather(norm_shifts, "shard", axis=1, tiled=True),
        lax.all_gather(qkv_spatial, "shard", axis=1, tiled=True),
        lax.all_gather(proj_spatial, "shard", axis=1, tiled=True),
        lax.all_gather(qkv_temporal, "shard", axis=1, tiled=True),
        lax.all_gather(proj_temporal, "shard", axis=1, tiled=True),
        lax.all_gather(up_weight, "shard", axis=0, tiled=True),
        lax.all_gather(down_weight, "shard", axis=1, tiled=True),
        lax.all_gather(out_bias, "shard", axis=1, tiled=True),
        lax.all_gather(qv_bias, "shard", axis=2, tiled=True),
        lax.all_gather(up_bias, "shard", axis=0, tiled=True),
    )
    (
        gain_rows,
        shift_rows,
        space_qkv,
        space_proj,
        time_qkv,
        time_proj,
        up_gathered,
        down_gathered,
        bias_rows,
        qv_here,
        up_here,
    ) = unpack(gathered, tp_rank, head_cols, hidden_cols)
    out_grad = cotangent.astype(jnp.float32)
    mlp_send = out_grad.astype(jnp.bfloat16)
    mlp_grad = spread_grads(mlp_send).reshape(row_count, model_width)
    grad_down = jnp.einsum("rh,rd->hd", hidden_act, mlp_grad, preferred_element_type=jnp.float32)
    grad_act = jnp.einsum("rd,hd->rh", mlp_grad, down_gathered, preferred_element_type=jnp.float32)
    _, act_pull = jax.vjp(activate, hidden_pre)
    grad_pre = act_pull(grad_act)[0].astype(jnp.bfloat16)
    grad_up = jnp.einsum("rd,rh->dh", mlp_normed, grad_pre, preferred_element_type=jnp.float32)
    grad_up_bias = jnp.sum(grad_pre, axis=0, dtype=jnp.float32)
    mlp_partial = jnp.einsum("rh,dh->rd", grad_pre, up_gathered, preferred_element_type=jnp.float32)
    _, norm_pull = jax.vjp(normalize, after_time, gain_rows[2], shift_rows[2])
    grad_mid, gain_mlp, shift_mlp = norm_pull(collect_grads(mlp_partial.reshape(full_shape)))
    time_grad_share = out_grad + grad_mid
    time_send = time_grad_share.astype(jnp.bfloat16)
    time_grad = spread_grads(time_send).reshape(row_count, model_width)
    grad_time_proj = jnp.einsum(
        "rc,rd->cd", time_out, time_grad, preferred_element_type=jnp.float32
    )
    time_out_grad = jnp.einsum(
        "rd,cd->rc", time_grad, time_proj, preferred_element_type=jnp.float32
    )
    time_out_grad = time_out_grad.astype(jnp.bfloat16).reshape(time_shape)
    grad_query, grad_keys, grad_values = attend_back(
        time_query, time_keys, time_values, time_total, time_out_grad, time_forms
    )
    grad_keys, grad_values = (
        lax.psum_scatter(
            grad_keys.astype(jnp.bfloat16), "ctx", scatter_dimension=1, tiled=True
        ).astype(jnp.float32),
        lax.psum_scatter(
            grad_values.astype(jnp.bfloat16), "ctx", scatter_dimension=1, tiled=True
        ).astype(jnp.float32),
    )
    time_grad_qkv = jnp.stack([grad_query, grad_keys, grad_values]).astype(jnp.bfloat16)
    time_grad_qkv = time_grad_qkv.reshape(3, row_count, head_cols)
    grad_time_qkv, grad_time_qv, time_partial = weight_side(time_normed, time_grad_qkv, time_qkv)
    _, norm_pull = jax.vjp(normalize, after_space, gain_rows[1], shift_rows[1])
    grad_mid, gain_time, shift_time = norm_pull(collect_grads(time_partial.reshape(full_shape)))
    space_grad_share = time_grad_share + grad_mid
    space_send = space_grad_share.astype(jnp.bfloat16)
    space_grad = spread_grads(space_send).reshape(row_count, model_width)
    grad_space_proj = jnp.einsum(
        "rc,rd->cd", space_out, space_grad, preferred_element_type=jnp.float32
    )
    space_out_grad = jnp.einsum(
        "rd,cd->rc", space_grad, space_proj, preferred_element_type=jnp.float32
    )
    space_out_grad = space_out_grad.astype(jnp.bfloat16).reshape(space_shape)
    grad_query, grad_keys, grad_values = attend_back(
        space_query, space_keys, space_values, space_total, space_out_grad, space_forms
    )
    space_grad_qkv = jnp.stack([grad_query, grad_keys, grad_values]).astype(jnp.bfloat16)
    space_grad_qkv = space_grad_qkv.reshape(3, row_count, head_cols)
    grad_space_qkv, grad_space_qv, space_partial = weight_side(
        space_normed, space_grad_qkv, space_qkv
    )
    _, norm_pull = jax.vjp(normalize, residual_in, gain_rows[0], shift_rows[0])
    grad_mid, gain_space, shift_space = norm_pull(collect_grads(space_partial.reshape(full_shape)))
    token_grad = space_grad_share + grad_mid
    sent_grads = (
        lax.psum_scatter(grad_space_qkv, ("shard", "ctx"), scatter_dimension=1, tiled=True),
        lax.psum_scatter(grad_space_proj, ("shard", "ctx"), scatter_dimension=1, tiled=True),
        lax.psum_scatter(grad_time_qkv, ("shard", "ctx"), scatter_dimension=1, tiled=True),
        lax.psum_scatter(grad_time_proj, ("shard", "ctx"), scatter_dimension=1, tiled=True),
        lax.psum_scatter(grad_up, ("shard", "ctx"), scatter_dimension=0, tiled=True),
        lax.psum_scatter(grad_down, ("shard", "ctx"), scatter_dimension=1, tiled=True),
    )
    qv_grad_whole = lax.dynamic_update_slice_in_dim(
        jnp.zeros((2, 2, model_width), jnp.float32),
        jnp.stack([grad_space_qv, grad_time_qv]),
        tp_rank * head_cols,
        2,
    )
    up_bias_whole = lax.dynamic_update_slice_in_dim(
        jnp.zeros((hidden_cols * tp_count,), jnp.float32), grad_up_bias, tp_rank * hidden_cols, 0
    )
    bias_grads = jnp.stack(
        [
            jnp.sum(space_send, axis=(0, 1, 2), dtype=jnp.float32),
            jnp.sum(time_send, axis=(0, 1, 2), dtype=jnp.float32),
            jnp.sum(mlp_send, axis=(0, 1, 2), dtype=jnp.float32),
        ]
    )
    vectors = (
        lax.psum_scatter(
            jnp.stack([gain_space, gain_time, gain_mlp]),
            ("shard", "ctx", "tp"),
            scatter_dimension=1,
            tiled=True,
        ),
        lax.psum_scatter(
            jnp.stack([shift_space, shift_time, shift_mlp]),
            ("shard", "ctx", "tp"),
            scatter_dimension=1,
            tiled=True,
        ),
        lax.psum_scatter(bias_grads, ("shard", "ctx", "tp"), scatter_dimension=1, tiled=True),
        lax.psum_scatter(qv_grad_whole, ("shard", "ctx", "tp"), scatter_dimension=2, tiled=True),
        lax.psum_scatter(up_bias_whole, ("shard", "ctx", "tp"), scatter_dimension=0, tiled=True),
    )
    return (
        finished.astype(jnp.bfloat16),
        token_grad,
        vectors[0],
        vectors[1],
        sent_grads[0],
        sent_grads[1],
        sent_grads[2],
        sent_grads[3],
        sent_grads[4],
        sent_grads[5],
        vectors[2],
        vectors[3],
        vectors[4],
    )


def solution(mesh):
    return jax.shard_map(
        on_device,
        mesh=mesh,
        in_specs=(
            P("shard", "ctx", "tp", None),
            P("shard", "ctx", "tp", None),
            P(None, "shard"),
            P(None, "shard"),
            P(None, "shard", "tp"),
            P("tp", "shard"),
            P(None, "shard", "tp"),
            P("tp", "shard"),
            P("shard", "tp"),
            P("tp", "shard"),
            P(None, "shard"),
            P(None, None, "shard"),
            P("shard"),
        ),
        out_specs=(
            P("shard", "ctx", "tp", None),
            P("shard", "ctx", "tp", None),
            P(None, ("shard", "ctx", "tp")),
            P(None, ("shard", "ctx", "tp")),
            P(None, ("shard", "ctx"), "tp"),
            P("tp", ("shard", "ctx")),
            P(None, ("shard", "ctx"), "tp"),
            P("tp", ("shard", "ctx")),
            P(("shard", "ctx"), "tp"),
            P("tp", ("shard", "ctx")),
            P(None, ("shard", "ctx", "tp")),
            P(None, None, ("shard", "ctx", "tp")),
            P(("shard", "ctx", "tp")),
        ),
        check_vma=False,
    )
```

profile of v0, /device:TPU:0, one launch (start us, length us, event | category | flops | bytes accessed | tf_op | source)
XLA Modules:
  0.0 1060.7 jit_solution(14277463233605368364)
XLA Ops:
  7.2 5.6 all_gather.64
  12.8 4.5 all_gather.65
  22.0 4.5 all_gather.68
  26.5 8.7 all_gather.69
  35.4 9.1 all_gather.67
  44.5 10.1 all-gather.12.cloned.1.call-done
  66.8 4.5 all_gather.70
  73.1 49.7 %all-reduce.19.cloned.1.call-done = bf16[1,4,196,768]{3,1,0,2:T(4,128)(2,1)} async-done(((bf16[1,4,196,768]{3,1,0,2:T(4,128)(2,1)}), bf16[1,4,196,768]{3,1,0,2:T(4,128)(2,1)}) %all-reduce.19.cloned.1.call-update) | async-done | bytes 1204240
  127.6 12.9 %all_gather.72 = bf16[3,768,192]{1,2,0:T(8,128)(2,1)} all-gather(bf16[3,384,192]{1,2,0:T(8,128)(2,1)S(1)} %copy-done.30), channel_id=1, replica_groups=mesh['shard'=2,'ctx'=4,'tp'=4] {'shard'}, dimensions={1}, use_global_device_ids=true | all-gather | bytes 1327104 | tf_op jit(solution)/shard_map/all_gather | solution.py:168
  140.5 17.6 %all-gather.14.cloned.1.call-done = bf16[1,4,196,768]{3,1,0,2:T(4,128)(2,1)} async-done(((bf16[1,4,49,768]{3,1,0,2:T(4,128)(2,1)}), bf16[1,4,196,768]{3,1,0,2:T(4,128)(2,1)}) %all-gather.14.cloned.1.call-update) | async-done | bytes 1204240 | tf_op jit(solution)/shard_map/all_gather | solution.py:83
  171.2 6.1 all_gather.75
  181.3 6.5 all-gather.18.cloned.1.call-done
  187.9 4.8 copy.97
  199.4 9.6 all-gather.16.cloned.1.call-done
  209.0 4.8 copy.95
  213.9 4.4 fusion.36
  223.5 56.2 %all-reduce.21.cloned.1.call-done = bf16[1,4,196,768]{3,1,0,2:T(4,128)(2,1)} async-done(((bf16[1,4,196,768]{3,1,0,2:T(4,128)(2,1)}), bf16[1,4,196,768]{3,1,0,2:T(4,128)(2,1)}) %all-reduce.21.cloned.1.call-update) | async-done | bytes 1204240
  284.6 4.7 all-gather
  292.7 19.1 %all-gather.26.cloned.1.call-done = bf16[1,4,196,768]{3,1,0,2:T(4,128)(2,1)} async-done(((bf16[1,4,49,768]{3,1,0,2:T(4,128)(2,1)}), bf16[1,4,196,768]{3,1,0,2:T(4,128)(2,1)}) %all-gather.26.cloned.1.call-update) | async-done | bytes 1204240 | tf_op jit(solution)/shard_map/all_gather | solution.py:93
  316.4 27.4 %all-gather.20.cloned.1.call-done = bf16[1,4,196,768]{3,1,0,2:T(4,128)(2,1)} async-done(((bf16[1,4,49,768]{3,1,0,2:T(4,128)(2,1)}), bf16[1,4,196,768]{3,1,0,2:T(4,128)(2,1)}) %all-gather.20.cloned.1.call-update) | async-done | bytes 1204240 | tf_op jit(solution)/shard_map/all_gather | solution.py:83
  348.6 18.8 %all-gather.22.cloned.1.call-done = bf16[768,768]{1,0:T(8,128)(2,1)} async-done(((bf16[384,768]{1,0:T(8,128)(2,1)}), bf16[768,768]{1,0:T(8,128)(2,1)}) %all-gather.22.cloned.1.call-update) | async-done | bytes 1179664 | tf_op jit(solution)/shard_map/all_gather | solution.py:170
  367.3 4.1 fusion.115
  371.5 20.1 %all-gather.24.cloned.1.call-done = bf16[768,768]{1,0:T(8,128)(2,1)} async-done(((bf16[768,384]{1,0:T(8,128)(2,1)}), bf16[768,768]{1,0:T(8,128)(2,1)}) %all-gather.24.cloned.1.call-update) | async-done | bytes 1179664 | tf_op jit(solution)/shard_map/all_gather | solution.py:171
  391.5 10.5 convert_reduce_fusion
  410.3 56.9 %all-reduce.23.cloned.1.call-done = bf16[1,4,196,768]{3,1,0,2:T(4,128)(2,1)} async-done(((bf16[1,4,196,768]{3,1,0,2:T(4,128)(2,1)}), bf16[1,4,196,768]{3,1,0,2:T(4,128)(2,1)}) %all-reduce.23.cloned.1.call-update) | async-done | bytes 1204240
  477.3 28.0 %all-gather.28.cloned.1.call-done = bf16[1,4,196,768]{3,1,0,2:T(4,128)(2,1)} async-done(((bf16[1,4,49,768]{3,1,0,2:T(4,128)(2,1)}), bf16[1,4,196,768]{3,1,0,2:T(4,128)(2,1)}) %all-gather.28.cloned.1.call-update) | async-done | bytes 1204240 | tf_op jit(solution)/shard_map/all_gather | solution.py:93
  517.1 5.8 convert_bitcast_fusion
  522.9 4.6 copy.114
  527.6 4.0 multiply_reduce_fusion.2
  536.4 4.6 copy.111
  550.9 4.1 reduce-scatter.23.cloned.1.call-done
  559.1 26.4 %reduce-scatter.21.cloned.1.call-done = bf16[1,4,196,3,64]{2,4,3,0,1:T(8,128)(2,1)} async-done(((bf16[1,16,196,3,64]{2,4,3,0,1:T(8,128)(2,1)}), bf16[1,4,196,3,64]{2,4,3,0,1:T(8,128)(2,1)}) %reduce-scatter.21.cloned.1.call-update) | async-done | bytes 301072 | tf_op jit(solution)/shard_map/reduce_scatter | solution.py:281
  593.2 4.1 dot_general.118
  601.6 56.9 %all-reduce.25.cloned.1.call-done = bf16[1,4,196,768]{3,1,0,2:T(4,128)(2,1)} async-done(((bf16[1,4,196,768]{3,1,0,2:T(4,128)(2,1)}), bf16[1,4,196,768]{3,1,0,2:T(4,128)(2,1)}) %all-reduce.25.cloned.1.call-update) | async-done | bytes 1204240
  663.5 3.7 convert_reduce_fusion.9
  677.1 3.9 convolution_bitcast_fusion
  681.0 4.2 copy.152
  685.2 4.7 reshape.486
  743.8 4.3 copy.148
  748.1 4.8 reshape.482
  753.0 4.2 fusion.117
  758.5 4.3 fusion.116
  765.7 12.9 %reduce-scatter.33.cloned.1.call-done = f32[96,576]{1,0:T(8,128)} async-done(((f32[768,576]{1,0:T(8,128)}), f32[96,576]{1,0:T(8,128)}) %reduce-scatter.33.cloned.1.call-update) | async-done | bytes 221200
  780.9 36.1 %reduce-scatter.31.cloned.1.call-done = f32[96,192]{1,0:T(8,128)} async-done(((f32[768,192]{1,0:T(8,128)}), f32[96,192]{1,0:T(8,128)}) %reduce-scatter.31.cloned.1.call-update) | async-done | bytes 73744
  818.7 98.5 %all-reduce.27.cloned.1.call-done = (bf16[1,4,196,768]{3,1,0,2:T(4,128)(2,1)}, bf16[1,4,196,768]{3,1,0,2:T(4,128)(2,1)}) async-done(((bf16[1,4,196,768]{3,1,0,2:T(4,128)(2,1)}, bf16[1,4,196,768]{3,1,0,2:T(4,128)(2,1)}), (bf16[1,4,196,768]{3,1,0,2:T(4,128)(2,1)}, bf16[1,4,196,768]{3,1,0,2:T(4,128)(2,1)})) %all-reduce.27.cloned.1.call-update) | async-done | bytes 2408464
  920.4 40.5 %all-reduce.11 = (f32[3,768]{1,0:T(4,128)S(1)}, f32[3,768]{1,0:T(4,128)S(1)}, f32[3,768]{1,0:T(4,128)S(1)}, f32[2,2,768]{2,1,0:T(2,128)S(1)}, f32[3072]{0:T(1024)S(1)}) all-reduce(f32[3,768]{1,0:T(4,128)S(1)} %get-tuple-element.116, ...), channel_id=10, replica_groups=mesh['shard'=2,'ctx'=4,'tp'=4] {'shard','ctx','tp'}, use_global_device_ids=true, to_apply=%region_29.0.clone | all-reduce | flops 13056 | bytes 104448
  968.6 38.7 %reduce-scatter.27.cloned.1.call-done = f32[768,96]{0,1:T(8,128)} async-done(((f32[768,768]{0,1:T(8,128)}), f32[768,96]{0,1:T(8,128)}) %reduce-scatter.27.cloned.1.call-update) | async-done | bytes 294928 | tf_op jit(solution)/shard_map/reduce_scatter | solution.py:320
  1007.3 46.5 %reduce-scatter.25.cloned.1.call-done = f32[96,768]{1,0:T(8,128)} async-done(((f32[768,768]{1,0:T(8,128)}), f32[96,768]{1,0:T(8,128)}) %reduce-scatter.25.cloned.1.call-update) | async-done | bytes 294928 | tf_op jit(solution)/shard_map/reduce_scatter | solution.py:319
  (330 shorter events, 217.4 us)
Async XLA Ops:
  7.2 28.2 %copy-start.29 = (bf16[3,384,192]{1,2,0:T(8,128)(2,1)S(1)}, bf16[3,384,192]{1,2,0:T(8,128)(2,1)}, u32[]{:S(2)}) copy-start(bf16[3,384,192]{1,2,0:T(8,128)(2,1)} %param.17) | copy-start | bytes 1327108
  7.2 47.5 %all-gather.12.cloned.1.call-start = ((), (), s32[]{:S(2)}) async-start(), calls=%async_computation.8 | async-start | bytes 1505280 | tf_op jit(solution)/shard_map/all_gather | solution.py:83
  19.8 24.7 %copy-start.33 = (f32[4,49]{0,1:T(8,128)}, f32[4,49]{0,1:T(8,128)S(1)}, u32[]{:S(2)}) copy-start(f32[4,49]{0,1:T(8,128)S(1)} %fusion.72) | copy-start | bytes 2356
  19.9 24.7 %copy-start.27 = (f32[4,49]{0,1:T(8,128)}, f32[4,49]{0,1:T(8,128)S(1)}, u32[]{:S(2)}) copy-start(f32[4,49]{0,1:T(8,128)S(1)} %fusion.98) | copy-start | bytes 2356
  21.9 100.9 %all-reduce.19.cloned.1.call-start = ((), (), s32[]{:S(2)}) async-start(), calls=%async_computation.26 | async-start | bytes 2408448
  65.2 6.1 copy-start.55
  65.2 57.6 %copy-start = (bf16[1,4,49,768]{3,1,2,0:T(4,128)(2,1)S(1)}, bf16[1,4,49,768]{3,1,2,0:T(4,128)(2,1)}, u32[]{:S(2)}) copy-start(bf16[1,4,49,768]{3,1,2,0:T(4,128)(2,1)} %param.13) | copy-start | bytes 903172
  66.7 60.9 %copy-start.30 = (bf16[3,384,192]{1,2,0:T(8,128)(2,1)S(1)}, bf16[3,384,192]{1,2,0:T(8,128)(2,1)}, u32[]{:S(2)}) copy-start(bf16[3,384,192]{1,2,0:T(8,128)(2,1)} %param.19) | copy-start | bytes 1327108
  66.7 91.4 %all-gather.14.cloned.1.call-start = ((), (), s32[]{:S(2)}) async-start(), calls=%async_computation.9 | async-start | bytes 1505280 | tf_op jit(solution)/shard_map/all_gather | solution.py:83
  125.4 35.3 %copy-start.35 = (f32[4,49]{0,1:T(8,128)}, f32[4,49]{0,1:T(8,128)S(1)}, u32[]{:S(2)}) copy-start(f32[4,49]{0,1:T(8,128)S(1)} %multiply_reduce_fusion.4) | copy-start | bytes 2356
  127.6 60.3 %all-gather.18.cloned.1.call-start = ((), (), s32[]{:S(2)}) async-start(), calls=%async_computation.11 | async-start | bytes 1966080 | tf_op jit(solution)/shard_map/all_gather | solution.py:210
  166.8 4.5 copy-start.39
  168.9 40.1 %all-gather.16.cloned.1.call-start = ((), (), s32[]{:S(2)}) async-start(), calls=%async_computation.10 | async-start | bytes 1966080 | tf_op jit(solution)/shard_map/all_gather | solution.py:211
  171.2 108.5 %all-reduce.21.cloned.1.call-start = ((), (), s32[]{:S(2)}) async-start(), calls=%async_computation.27 | async-start | bytes 2408448
  181.3 14.6 %copy-start.9 = (bf16[4,196,3,64]{3,0,2,1:T(4,128)(2,1)}, bf16[4,196,3,64]{3,0,2,1:T(4,128)(2,1)S(1)}, u32[]{:S(2)}) copy-start(bf16[4,196,3,64]{3,0,2,1:T(4,128)(2,1)S(1)} %copy.98) | copy-start | bytes 903172
  199.4 14.5 %copy-start.13 = (f32[196,3,4]{2,1,0:T(4,128)S(1)}, f32[196,3,4]{2,1,0:T(4,128)}, u32[]{:S(2)}) copy-start(f32[196,3,4]{2,1,0:T(4,128)} %copy-done.12) | copy-start | bytes 28228
  222.7 89.0 %all-gather.26.cloned.1.call-start = ((), (), s32[]{:S(2)}) async-start(), calls=%async_computation.15 | async-start | bytes 1505280 | tf_op jit(solution)/shard_map/all_gather | solution.py:93
  223.5 120.4 %all-gather.20.cloned.1.call-start = ((), (), s32[]{:S(2)}) async-start(), calls=%async_computation.12 | async-start | bytes 1505280 | tf_op jit(solution)/shard_map/all_gather | solution.py:83
  281.5 32.7 %copy-start.36 = (f32[4,49]{0,1:T(8,128)}, f32[4,49]{0,1:T(8,128)S(1)}, u32[]{:S(2)}) copy-start(f32[4,49]{0,1:T(8,128)S(1)} %multiply_reduce_fusion.3) | copy-start | bytes 2356
  282.5 84.8 %all-gather.22.cloned.1.call-start = ((), (), s32[]{:S(2)}) async-start(), calls=%async_computation.13 | async-start | bytes 1769472 | tf_op jit(solution)/shard_map/all_gather | solution.py:170
  283.3 108.3 %all-gather.24.cloned.1.call-start = ((), (), s32[]{:S(2)}) async-start(), calls=%async_computation.14 | async-start | bytes 1769472 | tf_op jit(solution)/shard_map/all_gather | solution.py:171
  283.9 183.4 %all-reduce.23.cloned.1.call-start = ((), (), s32[]{:S(2)}) async-start(), calls=%async_computation.28 | async-start | bytes 2408448
  292.7 98.9 %copy-start.48 = (f32[768]{0:T(1024)}, f32[768]{0:T(1024)S(1)}, u32[]{:S(2)}) copy-start(f32[768]{0:T(1024)S(1)} %dynamic-slice_convert_fusion) | copy-start | bytes 9220
  391.5 11.6 %copy-start.54 = (bf16[768,768]{1,0:T(8,128)(2,1)S(1)}, bf16[768,768]{1,0:T(8,128)(2,1)}, u32[]{:S(2)}) copy-start(bf16[768,768]{1,0:T(8,128)(2,1)} %all-gather.22.cloned.1.call-done) | copy-start | bytes 3538948
  410.3 95.1 %all-gather.28.cloned.1.call-start = ((), (), s32[]{:S(2)}) async-start(), calls=%async_computation.16 | async-start | bytes 1505280 | tf_op jit(solution)/shard_map/all_gather | solution.py:93
  467.3 4.5 copy-start.17
  474.8 80.2 %reduce-scatter.23.cloned.1.call-start = ((), (), s32[]{:S(2)}) async-start(), calls=%async_computation.18 | async-start | bytes 1966080 | tf_op jit(solution)/shard_map/reduce_scatter | solution.py:284
  527.5 58.0 %reduce-scatter.21.cloned.1.call-start = ((), (), s32[]{:S(2)}) async-start(), calls=%async_computation.17 | async-start | bytes 1966080 | tf_op jit(solution)/shard_map/reduce_scatter | solution.py:281
  541.0 117.5 %all-reduce.25.cloned.1.call-start = ((), (), s32[]{:S(2)}) async-start(), calls=%async_computation.29 | async-start | bytes 2408448
  601.6 104.1 %all-gather.30.cloned.1.call-start = ((), (), s32[]{:S(2)}) async-start(), calls=%async_computation.19 | async-start | bytes 1505280 | tf_op jit(solution)/shard_map/all_gather | solution.py:93
  658.5 4.9 copy-start.18
  658.5 4.9 copy-start.32
  667.2 96.5 %reduce-scatter.35.cloned.1.call-start = ((), (), s32[]{:S(2)}) async-start(), calls=%async_computation.25 | async-start | bytes 884736
  674.7 103.8 %reduce-scatter.33.cloned.1.call-start = ((), (), s32[]{:S(2)}) async-start(), calls=%async_computation.24 | async-start | bytes 2211840
  685.2 5.0 copy-start.38
  685.2 5.0 copy-start.41
  690.0 4.5 copy-start.49
  690.0 127.1 %reduce-scatter.31.cloned.1.call-start = ((), (), s32[]{:S(2)}) async-start(), calls=%async_computation.23 | async-start | bytes 884736
  724.8 4.8 copy-start.4
  729.6 187.6 %all-reduce.27.cloned.1.call-start = ((), (), s32[]{:S(2)}) async-start(), calls=%async_computation.30 | async-start | bytes 4816896
  738.8 227.9 %reduce-scatter.29.cloned.1.call-start = ((), (), s32[]{:S(2)}) async-start(), calls=%async_computation.22 | async-start | bytes 2211840
  748.1 4.9 copy-start.24
  753.0 254.3 %reduce-scatter.27.cloned.1.call-start = ((), (), s32[]{:S(2)}) async-start(), calls=%async_computation.21 | async-start | bytes 2654208 | tf_op jit(solution)/shard_map/reduce_scatter | solution.py:320
  757.2 296.5 %reduce-scatter.25.cloned.1.call-start = ((), (), s32[]{:S(2)}) async-start(), calls=%async_computation.20 | async-start | bytes 2654208 | tf_op jit(solution)/shard_map/reduce_scatter | solution.py:319
  765.3 153.3 %copy-start.34 = (f32[4,49]{0,1:T(8,128)S(1)}, f32[4,49]{0,1:T(8,128)}, u32[]{:S(2)}) copy-start(f32[4,49]{0,1:T(8,128)} %copy-done.33) | copy-start | bytes 2356
  765.3 153.3 %copy-start.28 = (f32[4,49]{0,1:T(8,128)S(1)}, f32[4,49]{0,1:T(8,128)}, u32[]{:S(2)}) copy-start(f32[4,49]{0,1:T(8,128)} %copy-done.27) | copy-start | bytes 2356
  765.6 198.5 %copy-start.19 = (f32[1,4,49,768]{3,1,0,2:T(4,128)S(1)}, f32[1,4,49,768]{3,1,0,2:T(4,128)}, u32[]{:S(2)}) copy-start(f32[1,4,49,768]{3,1,0,2:T(4,128)} %get-tuple-element.82) | copy-start | bytes 1806340
  765.7 198.5 %copy-start.50 = (f32[768]{0:T(1024)S(1)}, f32[768]{0:T(1024)}, u32[]{:S(2)}) copy-start(f32[768]{0:T(1024)} %get-tuple-element.61) | copy-start | bytes 9220
  (32 other events, 59.6 us)
Sparse Core Ops, SparseCore 0:
  22.0 32.5 all-gather.11
  66.9 55.8 all-reduce.18
  127.7 30.4 all-gather.13
  169.1 18.7 all-gather.17
  189.3 19.6 all-gather.15
  222.8 56.8 all-reduce.20
  281.2 30.4 all-gather.25
  313.9 29.9 all-gather.19
  345.4 21.8 all-gather.21
  368.7 22.7 all-gather.23
  410.4 56.8 all-reduce.22
  474.9 30.4 all-gather.27
  527.6 27.2 reduce-scatter.22
  557.3 28.1 reduce-scatter.20
  601.7 56.8 all-reduce.24
  667.3 30.4 all-gather.29
  700.8 34.0 reduce-scatter.34
  738.2 40.3 reduce-scatter.32
  782.0 34.9 reduce-scatter.30
  819.5 97.6 all-reduce.26
  920.6 39.8 reduce-scatter.28
  964.8 42.4 reduce-scatter.26
  1011.2 42.4 reduce-scatter.24
where the time goes:
time: 1070 us; the launch traced here: 1060 us
  waiting for transfers between devices  642 us (60%)
  local copies, waits for them, and re-layouts  164 us (15%)
  blocking collectives  101 us (9%)
  matrix products  88 us (8%)
  other arithmetic  46.8 us (4%)
  between operations  16.1 us (2%)
    unnamed x32, waiting for transfers between devices  369 us
    all_gather x3, waiting for transfers between devices, spread_rows(): return lax.all_gather(normed_share, 'tp', axis=2, tiled=True)  55.2 us
    all_gather x3, waiting for transfers between devices, spread_grads(): return lax.all_gather(grad_share, 'tp', axis=2, tiled=True)  47.1 us
    reduce_scatter x1, waiting for transfers between devices, on_device(): lax.psum_scatter(grad_up, ('shard', 'ctx'), scatter_dimension=0, tiled=True)  46.5 us
    unnamed x136, local copies, waits for them, and re-layouts  43.3 us
    unnamed x1, blocking collectives  40.5 us
    reduce_scatter x1, waiting for transfers between devices, on_device(): lax.psum_scatter(grad_down, ('shard', 'ctx'), scatter_dimension=1, tiled=...  38.7 us
    reduce_scatter x1, waiting for transfers between devices, on_device(): lax.psum_scatter(grad_keys.astype(jnp.bfloat16), 'ctx', scatter_dimension...  26.4 us
  transfers between devices with their start and end apart: 23, of which 20 were waited for; matrix products, arithmetic and copies ran while one was open for 16% of the time, Pallas kernels for 0%

commit v1 on v0

v1 whole, which is shorter than its diff:
```python
import functools

import jax
import jax.numpy as jnp
from jax import lax
from jax.experimental import pallas as pl
from jax.experimental.pallas import tpu as pltpu
from jax.sharding import PartitionSpec as P

HD = 64
EPS = 1e-06
SCALE = HD ** (-0.5)
SLOT = 16
bf16 = jnp.bfloat16
f32 = jnp.float32
VMEM = pl.BlockSpec(memory_space=pltpu.VMEM)
ANY = pl.BlockSpec(memory_space=pl.ANY)
LIMIT = 50 * 1024 * 1024


def nn(a, b):
    return lax.dot_general(a, b, (((1,), (0,)), ((), ())), preferred_element_type=f32)


def nt(a, b):
    return lax.dot_general(a, b, (((1,), (1,)), ((), ())), preferred_element_type=f32)


def tn(a, b):
    return lax.dot_general(a, b, (((0,), (0,)), ((), ())), preferred_element_type=f32)


def standardize(v):
    c = v - jnp.mean(v, axis=-1, keepdims=True)
    r = lax.rsqrt(jnp.mean(c * c, axis=-1, keepdims=True) + EPS)
    return c * r, r


def norm_back(d, q, r, gain):
    e = d * gain
    return r * (e - jnp.mean(e, axis=-1, keepdims=True) - q * jnp.mean(e * q, axis=-1, keepdims=True))


def softmax(q, k, mask):
    s = nt(q * jnp.asarray(SCALE, bf16), k) + mask
    e = jnp.exp(s - jnp.max(s, axis=-1, keepdims=True))
    return e / jnp.sum(e, axis=-1, keepdims=True)


def rows_of(refs):
    return jnp.concatenate([r[...].reshape(-1, r.shape[-1]) for r in refs], axis=0)


def put_rows(refs, value):
    n = value.shape[0] // len(refs)
    for i, r in enumerate(refs):
        r[...] = value[i * n : (i + 1) * n].reshape(r.shape).astype(r.dtype)


class Plan:
    def __init__(self, mesh, model, wide):
        self.sizes = (mesh.shape["shard"], mesh.shape["ctx"], mesh.shape["tp"])
        self.paired = self.sizes == (2, 4, 4)
        self.model, self.wide, self.blocks = model, wide, self.sizes[2]
        self.strips = 8 if self.paired else 1

    def ranks(self):
        return lax.axis_index("shard"), lax.axis_index("ctx"), lax.axis_index("tp")

    def gather(self, local):
        if not self.paired:
            full = lax.all_gather(local, "shard", axis=0, tiled=True)
            return [lax.all_gather(full, "tp", axis=1, tiled=True)[None]]
        rows = local.shape[0] // 4
        own = lax.dynamic_slice_in_dim(local, lax.axis_index("ctx") * rows, rows, 0)
        a = jnp.stack([own] + [shift_z(own, k) for k in (1, 2, 3)])
        x, y = flip_x(a), flip_y(a)
        d1, d2 = flip_x(y[:2]), flip_y(x[2:])
        mine = [a, x, y, d1, d2]
        return mine + [flip_core(v) for v in mine]

    def places(self):
        if not self.paired:
            return [(0, 0, 0, 0)]
        x, q, z = self.ranks()
        out = []
        rows = self.model // 8
        for core in (0, 1):
            for i, (dx, dq, ks) in enumerate(
                ((0, 0, range(4)), (1, 0, range(4)), (0, 2, range(4)), (1, 2, (0, 1)), (1, 2, (2, 3)))
            ):
                for n, k in enumerate(ks):
                    row = ((x ^ dx) * 4 + (q ^ dq ^ core)) * rows
                    col = lax.rem(z + (4 - k), 4) * self.wide
                    out.append((5 * core + i, n, pl.multiple_of(row, rows), pl.multiple_of(col, self.wide)))
        return out

    def start_loads(self, refs, whole, sems):
        copies = []
        for n, (i, k, row, col) in enumerate(self.places()):
            shape = refs[i].shape
            copies.append(
                pltpu.make_async_copy(
                    refs[i].at[k], whole.at[pl.ds(row, shape[1]), pl.ds(col, shape[2])], sems.at[n]
                )
            )
        for c in copies:
            c.start()
        return copies

    def n_loads(self):
        return 32 if self.paired else 1

    def grad_shapes(self):
        rows = self.model // self.strips
        if self.paired:
            return [jax.ShapeDtypeStruct((2, 2, 4, rows, self.wide), bf16)] * 2
        return [jax.ShapeDtypeStruct((1, 1, self.blocks, rows, self.wide), bf16)]

    def grad_scratch(self):
        rows = self.model // self.strips
        if self.paired:
            return pltpu.VMEM((self.blocks, 2, 2, 2, rows, self.wide), bf16)
        return pltpu.VMEM((self.blocks, 1, 1, 1, rows, self.wide), bf16)

    def n_stores(self):
        return self.blocks * (2 if self.paired else 1)

    def start_stores(self, j, value, held, outs, sems):
        value = value.astype(bf16)
        if not self.paired:
            held[j, 0, 0, 0] = value
            c = pltpu.make_async_copy(held.at[j, 0], outs[0].at[:, :, j], sems.at[j])
            c.start()
            return [c]
        x, q, z = self.ranks()
        rows = self.model // 8
        for i in range(8):
            at = q ^ (i & 3)
            held[j, at & 1, at >> 1, x ^ (i >> 2)] = value[i * rows : (i + 1) * rows]
        slot = lax.rem(j + 4 - z, 4)
        copies = []
        for core in (0, 1):
            copies.append(
                pltpu.make_async_copy(held.at[j, core], outs[core].at[:, :, slot], sems.at[2 * j + core])
            )
            copies[-1].start()
        return copies

    def reduce(self, outs):
        if not self.paired:
            g = outs[0][0, 0].astype(f32)
            g = lax.psum_scatter(g, ("shard", "ctx"), scatter_dimension=1, tiled=True)
            return lax.psum_scatter(g, "tp", scatter_dimension=0, tiled=True)[0]
        keep, send = outs
        got = flip_core(send)

        def add(u, v):
            return (u.astype(f32) + v.astype(f32)).astype(bf16)

        send_a = add(keep[:, 1, :2], got[:, 1, :2])
        send_b = add(keep[1, :, 2:], got[1, :, 2:])
        got_a, got_b = flip_x(send_a), flip_y(send_b)
        keep_a = add(keep[:, 0, :2], got[:, 0, :2])
        keep_b = add(keep[0, :, 2:], got[0, :, 2:])
        next_a = add(keep_a[1], got_a[1])
        next_b = add(keep_b[1], got_b[1])
        last_a, last_b = flip_y(next_a), flip_x(next_b)

        def total(u, v, w):
            return u.astype(f32) + v.astype(f32) + w.astype(f32)

        parts = [total(keep_a[0, i], got_a[0, i], last_a[i]) for i in (0, 1)]
        parts += [total(keep_b[0, i], got_b[0, i], last_b[i]) for i in (0, 1)]
        out = parts[0]
        for k in (1, 2, 3):
            out = out + shift_z(parts[k].astype(bf16), k).astype(f32)
        return out


def flip_x(v):
    return lax.ppermute(v, "shard", [(i, i ^ 1) for i in range(2)])


def flip_ctx(v, e):
    return lax.ppermute(v, "ctx", [(i, i ^ e) for i in range(4)])


def flip_core(v):
    return flip_ctx(v, 1)


def flip_y(v):
    return flip_ctx(v, 2)


def shift_z(v, k):
    return lax.ppermute(v, "tp", [(i, (i + k) % 4) for i in range(4)])


def lay_out_kernel(x_ref, c_ref, *outs):
    z, q = lax.axis_index("tp"), lax.axis_index("ctx")
    xs, cs = outs
    for ref, out in ((x_ref, xs), (c_ref, cs)):
        patches = ref.shape[1]
        step = -(-patches // 4)
        for f in range(4):
            v = ref[f].astype(f32)
            for b in range(4):
                part = v[b * step : min((b + 1) * step, patches)]
                part = jnp.concatenate(
                    [part, jnp.zeros((SLOT - part.shape[0], part.shape[1]), f32)], axis=0
                )
                out[lax.rem(f + 4 - z, 4), b ^ q] = part.astype(out.dtype)


def lay_out(x, c):
    shape = jax.ShapeDtypeStruct((4, 4, SLOT, x.shape[-1]), bf16)
    return pl.pallas_call(
        lay_out_kernel,
        out_shape=[shape, shape],
        in_specs=[VMEM] * 2,
        out_specs=[VMEM] * 2,
        compiler_params=pltpu.CompilerParams(vmem_limit_bytes=LIMIT),
        name="lay_out",
    )(x, c)


def bring_back(parts, frames_first, patches, dtype):
    width = parts[0].shape[-1]

    def kernel(*refs):
        z, q = lax.axis_index("tp"), lax.axis_index("ctx")
        ins, out, held = refs[:4], refs[4], refs[5]
        step = -(-patches // 4)
        for i, r in enumerate(ins):
            if frames_first:
                held[i] = r[...].astype(f32)
            else:
                held[:, i] = r[...].astype(f32)
        for f in range(4):
            s = lax.rem(f + 4 - z, 4)
            rows = [held[s, b ^ q][: min(step, patches - b * step)] for b in range(4)]
            out[f] = jnp.concatenate(rows, axis=0).astype(out.dtype)

    return pl.pallas_call(
        kernel,
        out_shape=jax.ShapeDtypeStruct((4, patches, width), dtype),
        in_specs=[VMEM] * 4,
        out_specs=VMEM,
        scratch_shapes=[pltpu.VMEM((4, 4, SLOT, width), f32)],
        compiler_params=pltpu.CompilerParams(vmem_limit_bytes=LIMIT),
        name="bring_back",
    )(*parts)


def turn(parts):
    def kernel(*refs):
        for i in range(4):
            for k in range(4):
                refs[4 + k][i] = refs[i][k]

    shape = jax.ShapeDtypeStruct(parts[0].shape, parts[0].dtype)
    return pl.pallas_call(
        kernel,
        out_shape=[shape] * 4,
        in_specs=[VMEM] * 4,
        out_specs=[VMEM] * 4,
        compiler_params=pltpu.CompilerParams(vmem_limit_bytes=LIMIT),
        name="turn",
    )(*parts)


def swap_z_out(parts):
    return [parts[0]] + [shift_z(parts[k], k) for k in (1, 2, 3)]


def swap_z_back(parts):
    return [parts[0]] + [shift_z(parts[k], 4 - k) for k in (1, 2, 3)]


def swap_ctx(parts):
    return [parts[0]] + [flip_ctx(parts[e], e) for e in (1, 2, 3)]


def time_mask(rows):
    a = lax.broadcasted_iota(jnp.int32, (rows, rows), 0)
    b = lax.broadcasted_iota(jnp.int32, (rows, rows), 1)
    return jnp.where(((a ^ b) & (SLOT - 1)) == 0, 0.0, -1e30).astype(f32)


def attention_forward(plan, timed, head_cols):
    heads = head_cols // HD
    three = 3 * head_cols

    def kernel(*refs):
        refs = list(refs)

        def take(n):
            got, refs[:] = refs[:n], refs[n:]
            return got

        x_refs = take(4)
        b_refs = take(4) if timed else []
        (gain, shift, qv, mask_ref, bias_in) = take(5)
        w_refs = take(10 if plan.paired else 1)
        (p_ref, o_ref) = take(2)
        outs = take(2) if timed else take(4)
        whole, sems = take(2)
        loads = plan.start_loads(w_refs, whole, sems)
        x = rows_of(x_refs).astype(f32)
        if timed:
            x = x + rows_of(b_refs).astype(f32) + bias_in[0:1]
            outs[0][...] = x
            mask = time_mask(x.shape[0])
        else:
            mask = mask_ref[...]
        q, _ = standardize(x)
        n = (q * gain[...] + shift[...]).astype(bf16)
        for c in loads:
            c.wait()
        total = jnp.zeros(x.shape, f32)
        for j in range(plan.blocks):
            at = j * plan.wide
            p = (nn(n, whole[:, at : at + three]) + qv[j : j + 1]).astype(bf16)
            p_ref[j] = p
            attended = []
            for h in range(heads):
                qh = p[:, h * HD : (h + 1) * HD]
                kh = p[:, head_cols + h * HD : head_cols + (h + 1) * HD]
                vh = p[:, 2 * head_cols + h * HD : 2 * head_cols + (h + 1) * HD]
                attended.append(nn(softmax(qh, kh, mask).astype(bf16), vh))
            o = jnp.concatenate(attended, axis=-1).astype(bf16)
            o_ref[j] = o
            total = total + nt(o, whole[:, at + three : at + plan.wide])
        if timed:
            outs[1][...] = x + total + bias_in[1:2]
        else:
            put_rows(outs, total)

    return kernel


def attention_backward(plan, timed, head_cols):
    heads = head_cols // HD
    three = 3 * head_cols

    def kernel(*refs):
        refs = list(refs)

        def take(n):
            got, refs[:] = refs[:n], refs[n:]
            return got

        if timed:
            (x_ref, g_ref) = take(2)
        else:
            x_refs, g_refs = take(4), take(4)
        (gain, shift, mask_ref, p_ref, o_ref) = take(5)
        w_refs = take(10 if plan.paired else 1)
        grads = take(len(plan.grad_shapes()))
        sums, qv_sums = take(2)
        outs = take(4)
        whole, sems, held, out_sems = take(4)
        loads = plan.start_loads(w_refs, whole, sems)
        if timed:
            x, g = x_ref[...], g_ref[...]
            mask = time_mask(x.shape[0])
        else:
            x, g = rows_of(x_refs).astype(f32), rows_of(g_refs).astype(f32)
            mask = mask_ref[...]
        q, r = standardize(x)
        n_t = (q * gain[...] + shift[...]).T.astype(bf16)
        g_b = g.astype(bf16)
        g_t = g_b.astype(f32).T.astype(bf16)
        sums[2:3] = jnp.sum(g_b.astype(f32), axis=0, keepdims=True)
        for c in loads:
            c.wait()
        d_n = jnp.zeros(x.shape, f32)
        stores = []
        for j in range(plan.blocks):
            at = j * plan.wide
            p, o = p_ref[j], o_ref[j]
            d_o = nn(g_b, whole[:, at + three : at + plan.wide]).astype(bf16)
            d_q, d_k, d_v = [], [], []
            for h in range(heads):
                qh = p[:, h * HD : (h + 1) * HD]
                kh = p[:, head_cols + h * HD : head_cols + (h + 1) * HD]
                vh = p[:, 2 * head_cols + h * HD : 2 * head_cols + (h + 1) * HD]
                doh = d_o[:, h * HD : (h + 1) * HD]
                w = softmax(qh, kh, mask)
                d_v.append(tn(w.astype(bf16), doh))
                d_w = nt(doh, vh)
                inner = jnp.sum(d_w * w, axis=-1, keepdims=True)
                d_s = (w * (d_w - inner)).astype(bf16)
                d_q.append(nn(d_s, kh) * SCALE)
                d_k.append(tn(d_s, qh) * SCALE)
            d_p = jnp.concatenate(d_q + d_k + d_v, axis=-1).astype(bf16)
            qv_sums[j : j + 1] = jnp.sum(d_p.astype(f32), axis=0, keepdims=True)
            block = jnp.concatenate([nn(n_t, d_p), nn(g_t, o)], axis=-1)
            stores += plan.start_stores(j, block, held, grads, out_sems)
            d_n = d_n + nt(d_p, whole[:, at : at + three])
        sums[0:1] = jnp.sum(d_n * q, axis=0, keepdims=True)
        sums[1:2] = jnp.sum(d_n, axis=0, keepdims=True)
        put_rows(outs, g + norm_back(d_n, q, r, gain[...]))
        for c in stores:
            c.wait()

    return kernel


def mlp_kernel(plan):
    def kernel(*refs):
        refs = list(refs)

        def take(n):
            got, refs[:] = refs[:n], refs[n:]
            return got

        (x_ref,) = take(1)
        g_refs = take(4)
        gain, shift, up_bias, out_bias = take(4)
        n_w = 10 if plan.paired else 1
        up_refs, down_refs = take(n_w), take(n_w)
        n_g = len(plan.grad_shapes())
        up_grads, down_grads = take(n_g), take(n_g)
        sums, up_sums, back = take(3)
        outs = take(4)
        up, down, up_sem, down_sem, up_held, down_held, up_out, down_out = take(8)
        up_loads = plan.start_loads(up_refs, up, up_sem)
        down_loads = plan.start_loads(down_refs, down, down_sem)
        x = x_ref[...]
        g = rows_of(g_refs)
        g_t = g.astype(f32).T.astype(bf16)
        q, r = standardize(x)
        n32 = q * gain[...] + shift[...]
        n, n_t = n32.astype(bf16), n32.T.astype(bf16)
        for c in up_loads + down_loads:
            c.wait()
        total = jnp.zeros(x.shape, f32)
        d_n = jnp.zeros(x.shape, f32)
        stores = []
        for j in range(plan.blocks):
            cols = slice(j * plan.wide, (j + 1) * plan.wide)
            u = nn(n, up[:, cols]) + up_bias[j : j + 1]
            half = 0.5 * (1.0 + lax.erf(u * (0.5**0.5)))
            z = (u * half).astype(bf16)
            slope = half + u * (jnp.exp(-0.5 * u * u) * 0.3989422804014327)
            d_u = (nn(g, down[:, cols]) * slope).astype(bf16)
            stores += plan.start_stores(j, nn(g_t, z), down_held, down_grads, down_out)
            stores += plan.start_stores(j, nn(n_t, d_u), up_held, up_grads, up_out)
            total = total + nt(z, down[:, cols])
            d_n = d_n + nt(d_u, up[:, cols])
            up_sums[j : j + 1] = jnp.sum(d_u.astype(f32), axis=0, keepdims=True)
        put_rows(outs, x + total + out_bias[...])
        sums[0:1] = jnp.sum(d_n * q, axis=0, keepdims=True)
        sums[1:2] = jnp.sum(d_n, axis=0, keepdims=True)
        sums[2:3] = jnp.sum(g.astype(f32), axis=0, keepdims=True)
        back[...] = g.astype(f32) + norm_back(d_n, q, r, gain[...])
        for c in stores:
            c.wait()

    return kernel


def call(kernel, ins, n_any, outs, n_any_out, scratch, name, flops, any_first=False):
    moved = sum(v.size * v.dtype.itemsize for v in list(ins) + list(outs))
    return pl.pallas_call(
        kernel,
        out_shape=outs,
        in_specs=[VMEM] * (len(ins) - n_any) + [ANY] * n_any,
        out_specs=[ANY] * n_any_out + [VMEM] * (len(outs) - n_any_out),
        scratch_shapes=scratch,
        compiler_params=pltpu.CompilerParams(vmem_limit_bytes=LIMIT),
        cost_estimate=pl.CostEstimate(flops=flops, bytes_accessed=moved, transcendentals=0),
        name=name,
    )(*ins)


def on_device(
    mesh,
    tokens,
    cotangent,
    norm_gains,
    norm_shifts,
    qkv_spatial,
    proj_spatial,
    qkv_temporal,
    proj_temporal,
    up_weight,
    down_weight,
    out_bias,
    qv_bias,
    up_bias,
):
    shards = mesh.shape["shard"]
    blocks = mesh.shape["tp"]
    patches, model = tokens.shape[2:]
    head_cols = qkv_spatial.shape[2]
    wide = 4 * head_cols
    rows = 16 * SLOT
    plan = Plan(mesh, model, wide)
    x_rank, q_rank, z_rank = plan.ranks()

    part = norm_gains.shape[1]
    n_up = up_bias.shape[0] // part
    small = jnp.concatenate(
        [norm_gains, norm_shifts, out_bias, qv_bias.reshape(-1, part), up_bias.reshape(n_up, part)], axis=0
    )
    if plan.paired:
        other = flip_x(small)
        first = jnp.where(x_rank == 0, small, other)
        second = jnp.where(x_rank == 0, other, small)
        small = jnp.stack([first, second])
    else:
        small = lax.all_gather(small, "shard", axis=0, tiled=False)
    small = small.astype(f32)
    vectors = jnp.swapaxes(small[:, :13], 0, 1).reshape(13, model)
    gains, shifts, biases = vectors[0:3], vectors[3:6], vectors[6:9]
    qv = vectors[9:13].reshape(2, 2, blocks, head_cols)
    qv = jnp.concatenate([qv[:, 0], jnp.zeros_like(qv[:, 0]), qv[:, 1]], axis=-1)
    up_b = small[:, 13:].reshape(blocks, -1)

    def joined(qkv, proj):
        return jnp.concatenate([qkv[0], qkv[1], qkv[2], proj.T], axis=1)

    w_space = plan.gather(joined(qkv_spatial, proj_spatial))
    w_time = plan.gather(joined(qkv_temporal, proj_temporal))
    w_up = plan.gather(up_weight)
    w_down = plan.gather(down_weight.T)
    n_w = len(w_space)

    laid, cot = lay_out(tokens[0], cotangent[0])
    by_patch = [v.reshape(4 * SLOT, model) for v in swap_z_out([laid[s] for s in range(4)])]
    by_frame = swap_ctx([laid[:, e] for e in range(4)])
    cot_frame = swap_ctx([cot[:, e] for e in range(4)])

    step = -(-patches // 4)
    slot = jnp.arange(SLOT)[None, :]
    block = (jnp.arange(4) ^ q_rank)[:, None]
    valid = (slot < step) & (block * step + slot < patches)
    key_mask = jnp.where(valid, 0.0, -1e30).astype(f32).reshape(1, 4 * SLOT)
    key_mask = jnp.tile(key_mask, (1, 4))

    weight_scratch = [pltpu.VMEM((model, blocks * wide), bf16), pltpu.SemaphoreType.DMA((plan.n_loads(),))]
    grad_scratch = [plan.grad_scratch(), pltpu.SemaphoreType.DMA((plan.n_stores(),))]
    grads = plan.grad_shapes()
    p_shape = jax.ShapeDtypeStruct((blocks, rows, 3 * head_cols), bf16)
    o_shape = jax.ShapeDtypeStruct((blocks, rows, head_cols), bf16)
    full = jax.ShapeDtypeStruct((rows, model), f32)
    unit = jax.ShapeDtypeStruct((4, SLOT, model), bf16)
    unit32 = jax.ShapeDtypeStruct((4, SLOT, model), f32)
    sums = jax.ShapeDtypeStruct((3, model), f32)
    qv_sums = jax.ShapeDtypeStruct((blocks, 3 * head_cols), f32)
    proj_flops = 2 * rows * model * wide * blocks

    p1, o1, *branch = call(
        attention_forward(plan, False, head_cols),
        by_patch + [gains[0:1], shifts[0:1], qv[0], key_mask, biases[0:2]] + w_space,
        n_w,
        [p_shape, o_shape] + [unit] * 4,
        0,
        weight_scratch,
        "space_forward",
        2 * proj_flops,
    )
    branch = swap_ctx(turn(swap_z_back(branch)))
    p2, o2, x1, x2 = call(
        attention_forward(plan, True, head_cols),
        by_frame + branch + [gains[1:2], shifts[1:2], qv[1], key_mask, biases[0:2]] + w_time,
        n_w,
        [p_shape, o_shape, full, full],
        0,
        weight_scratch,
        "time_forward",
        2 * proj_flops,
    )
    n_g = len(grads)
    got = call(
        mlp_kernel(plan),
        [x2] + cot_frame + [gains[2:3], shifts[2:3], up_b, biases[2:3]] + w_up + w_down,
        2 * n_w,
        grads + grads + [sums, jax.ShapeDtypeStruct((blocks, wide), f32), full] + [unit] * 4,
        2 * n_g,
        weight_scratch[:1] * 2 + weight_scratch[1:] * 2 + grad_scratch[:1] * 2 + grad_scratch[1:] * 2,
        "mlp",
        6 * proj_flops,
    )
    g_up, g_down = got[:n_g], got[n_g : 2 * n_g]
    mlp_sums, up_sums, g2 = got[2 * n_g : 2 * n_g + 3]
    finished = bring_back(swap_ctx(got[2 * n_g + 3 :]), False, patches, bf16)
    sum_down = plan.reduce(g_down)
    sum_up = plan.reduce(g_up)

    got = call(
        attention_backward(plan, True, head_cols),
        [x1, g2, gains[1:2], shifts[1:2], key_mask, p2, o2] + w_time,
        n_w,
        grads + [sums, qv_sums] + [unit] * 4,
        n_g,
        weight_scratch + grad_scratch,
        "time_backward",
        3 * proj_flops,
    )
    g_time, time_sums, time_qv = got[:n_g], got[n_g], got[n_g + 1]
    g1 = swap_z_out(turn(swap_ctx(got[n_g + 2 :])))
    sum_time = plan.reduce(g_time)

    got = call(
        attention_backward(plan, False, head_cols),
        by_patch + g1 + [gains[0:1], shifts[0:1], key_mask, p1, o1] + w_space,
        n_w,
        grads + [sums, qv_sums] + [unit32] * 4,
        n_g,
        weight_scratch + grad_scratch,
        "space_backward",
        3 * proj_flops,
    )
    g_space, space_sums, space_qv = got[:n_g], got[n_g], got[n_g + 1]
    token_grad = bring_back(swap_z_back(got[n_g + 2 :]), True, patches, f32)
    sum_space = plan.reduce(g_space)

    stacked = jnp.stack([space_sums, time_sums, mlp_sums], axis=1).reshape(9, model)
    qv_all = jnp.stack([space_qv, time_qv]).reshape(2, blocks, 3, head_cols)
    qv_all = jnp.swapaxes(qv_all[:, :, ::2], 1, 2).reshape(4, model)
    vector = jnp.concatenate([stacked, qv_all, up_sums.reshape(-1, model)], axis=0)
    if plan.paired:
        for e in (1, 2):
            vector = vector + flip_ctx(vector, e)
        vector = vector + flip_x(vector)
        for e in (1, 2):
            vector = vector + lax.ppermute(vector, "tp", [(i, i ^ e) for i in range(4)])
    else:
        vector = lax.psum(vector, ("shard", "ctx", "tp"))
    place = (x_rank * mesh.shape["ctx"] + q_rank) * blocks + z_rank
    many = shards * mesh.shape["ctx"] * blocks
    mine = lax.dynamic_slice_in_dim(vector[:13], place * (model // many), model // many, 1)
    hidden = vector[13:].reshape(-1)
    hidden = lax.dynamic_slice_in_dim(hidden, place * (hidden.shape[0] // many), hidden.shape[0] // many, 0)

    def apart(total):
        three = total[:, : 3 * head_cols].reshape(-1, 3, head_cols)
        return jnp.swapaxes(three, 0, 1), total[:, 3 * head_cols :].T

    qkv_space, proj_space = apart(sum_space)
    qkv_time, proj_time = apart(sum_time)
    return (
        finished[None],
        token_grad[None],
        mine[0:3],
        mine[3:6],
        qkv_space,
        proj_space,
        qkv_time,
        proj_time,
        sum_up,
        sum_down.T,
        mine[6:9],
        mine[9:13].reshape(2, 2, -1),
        hidden,
    )


def solution(mesh):
    return jax.shard_map(
        functools.partial(on_device, mesh),
        mesh=mesh,
        in_specs=(
            P("shard", "ctx", "tp", None),
            P("shard", "ctx", "tp", None),
            P(None, "shard"),
            P(None, "shard"),
            P(None, "shard", "tp"),
            P("tp", "shard"),
            P(None, "shard", "tp"),
            P("tp", "shard"),
            P("shard", "tp"),
            P("tp", "shard"),
            P(None, "shard"),
            P(None, None, "shard"),
            P("shard"),
        ),
        out_specs=(
            P("shard", "ctx", "tp", None),
            P("shard", "ctx", "tp", None),
            P(None, ("shard", "ctx", "tp")),
            P(None, ("shard", "ctx", "tp")),
            P(None, ("shard", "ctx"), "tp"),
            P("tp", ("shard", "ctx")),
            P(None, ("shard", "ctx"), "tp"),
            P("tp", ("shard", "ctx")),
            P(("shard", "ctx"), "tp"),
            P("tp", ("shard", "ctx")),
            P(None, ("shard", "ctx", "tp")),
            P(None, None, ("shard", "ctx", "tp")),
            P(("shard", "ctx", "tp")),
        ),
        check_vma=False,
    )
```

time: 1070 us -> 473 us (0.44)
  waiting for transfers between devices: 642 us -> 186 us
  starting transfers between devices: 2.05 us -> 123 us
  blocking collectives: 101 us -> 0 us
  local copies, waits for them, and re-layouts: 164 us -> 64.7 us
  matrix products: 88 us -> 0 us
  Pallas kernels: 0 us -> 65.5 us
  other arithmetic: 46.8 us -> 26.3 us
  between operations: 16.1 us -> 2.64 us
    unnamed x32 -> x0, waiting for transfers between devices: 369 us -> none
    ppermute x0 -> x113, waiting for transfers between devices: none -> 186 us  [the longest x36 68.2 us: shift_z(): return lax.ppermute(v, 'tp', [(i, (i + k) % 4) for i in range(4)])]
    all_gather x10 -> x0, waiting for transfers between devices: 157 us -> none  [the longest x3 55.2 us: spread_rows(): return lax.all_gather(normed_share, 'tp', axis=2, tiled=True)]
    ppermute x0 -> x113, starting transfers between devices: none -> 123 us  [the longest x36 70.8 us: shift_z(): return lax.ppermute(v, 'tp', [(i, (i + k) % 4) for i in range(4)])]
    reduce_scatter x4 -> x0, waiting for transfers between devices: 116 us -> none  [the longest x1 46.5 us: on_device(): lax.psum_scatter(grad_up, ('shard', 'ctx'), scatter_dimension=0, tiled=True)]
    dot_general x26 -> x0, matrix products: 77.2 us -> none  [the longest x1 10.5 us: on_device(): jnp.einsum('rd,hd->rh', mlp_grad, down_gathered, preferred_element_type=j...]
    pallas_call x0 -> x10, Pallas kernels: none -> 65.5 us  [the longest x5 65 us: call(): pl.pallas_call(kernel, out_shape=outs, in_specs=[VMEM] * (len(ins) - n_an...]
    all_gather x9 -> x0, blocking collectives: 60.6 us -> none  [the longest x1 12.9 us: on_device(): lax.all_gather(qkv_temporal, 'shard', axis=1, tiled=True)]
  transfers between devices with their start and end apart: 23 -> 113, of which waited for: 20 -> 49; matrix products, arithmetic and copies ran while one was open for 16% -> 10% of each run, Pallas kernels for 0% -> 11%
where the time goes in v1:
time: 473 us; the launch traced here: 467 us
  waiting for transfers between devices  186 us (39%)
  starting transfers between devices  123 us (26%)
  Pallas kernels  65.5 us (14%)
  local copies, waits for them, and re-layouts  64.7 us (14%)
  other arithmetic  26.3 us (6%)
    ppermute x36, starting transfers between devices, shift_z(): return lax.ppermute(v, 'tp', [(i, (i + k) % 4) for i in range(4)])  70.8 us
    ppermute x36, waiting for transfers between devices, shift_z(): return lax.ppermute(v, 'tp', [(i, (i + k) % 4) for i in range(4)])  68.2 us
    pallas_call x5, Pallas kernels, call(): pl.pallas_call(kernel, out_shape=outs, in_specs=[VMEM] * (len(ins) - n_an...  65 us
    ppermute x57, waiting for transfers between devices, flip_ctx(): return lax.ppermute(v, 'ctx', [(i, i ^ e) for i in range(4)])  60.3 us
    ppermute x18, waiting for transfers between devices, flip_x(): return lax.ppermute(v, 'shard', [(i, i ^ 1) for i in range(2)])  49.6 us
    unnamed x261, local copies, waits for them, and re-layouts  45.1 us
    ppermute x57, starting transfers between devices, flip_ctx(): return lax.ppermute(v, 'ctx', [(i, i ^ e) for i in range(4)])  29.3 us
    ppermute x18, starting transfers between devices, flip_x(): return lax.ppermute(v, 'shard', [(i, i ^ 1) for i in range(2)])  22.4 us
  transfers between devices with their start and end apart: 113, of which 49 were waited for; matrix products, arithmetic and copies ran while one was open for 10% of the time, Pallas kernels for 11%

profile of v1, /device:TPU:0, one launch (start us, length us, event | category | flops | bytes accessed | tf_op | source)
XLA Modules:
  0.0 467.2 jit_solution(6202976623502310958)
XLA Ops:
  2.7 3.1 collective-permute-start.7
  5.8 2.6 collective-permute-start.8
  14.3 2.7 collective-permute-start.5
  18.9 6.4 %collective-permute-start.3 = (bf16[4,16,768]{2,1,0:T(8,128)(2,1)S(1)}, bf16[4,16,768]{2,1,0:T(8,128)(2,1)S(1)}, u32[]{:S(2)}, u32[]{:S(2)}) collective-permute-start(bf16[4,16,768]{2,1,0:T(8,128)(2,1)S(1)} %get-tuple-element.169), channel_id=1, source_target_pairs={{0,1},{1,2},{2,3},{3,0},{4,5},{5,6},{6,7},{7,4},{8,9},{9,10},{10,1... | collective-permute-start | bytes 294920 | tf_op jit(solution)/shard_map/ppermute | solution.py:198
  35.6 12.2 %collective-permute-done.38.refs_3_ = bf16[4,16,768]{2,1,0:T(8,128)(2,1)S(1)} collective-permute-done((bf16[4,16,768]{2,1,0:T(8,128)(2,1)}, bf16[4,16,768]{2,1,0:T(8,128)(2,1)S(1)}, u32[]{:S(2)}, u32[]{:S(2)}) %collective-permute-start.38) | collective-permute-done | bytes 98336 | tf_op jit(solution)/shard_map/ppermute | solution.py:186
  47.8 3.4 collective-permute-start.26
  54.5 3.5 collective-permute-done.26
  58.7 3.9 collective-permute-done.27
  62.5 3.4 collective-permute-start.54
  65.9 5.5 %collective-permute-start.40 = (bf16[96,768]{1,0:T(8,128)(2,1)S(1)}, bf16[96,768]{1,0:T(8,128)(2,1)S(1)}, u32[]{:S(2)}, u32[]{:S(2)}) collective-permute-start(bf16[96,768]{1,0:T(8,128)(2,1)S(1)} %constant_dynamic-slice_fusion.1), channel_id=1, source_target_pairs={{0,1},{1,2},{2,3},{3,0},{4,5},{5,6},{6,7},{7,4},{8,9},{9,10},{10,1... | collective-permute-start | bytes 442376 | tf_op jit(solution)/shard_map/ppermute | solution.py:198
  75.3 2.7 collective-permute-start.42
  78.3 5.1 %collective-permute-done.41 = bf16[96,768]{1,0:T(8,128)(2,1)S(1)} collective-permute-done((bf16[96,768]{1,0:T(8,128)(2,1)S(1)}, bf16[96,768]{1,0:T(8,128)(2,1)S(1)}, u32[]{:S(2)}, u32[]{:S(2)}) %collective-permute-start.41) | collective-permute-done | bytes 147488 | tf_op jit(solution)/shard_map/ppermute | solution.py:198
  89.5 10.1 %collective-permute-done.29.refs_15_.refs_9_ = bf16[4,96,768]{2,1,0:T(8,128)(2,1)S(1)} collective-permute-done((bf16[4,96,768]{2,1,0:T(8,128)(2,1)S(1)}, bf16[4,96,768]{2,1,0:T(8,128)(2,1)S(1)}, u32[]{:S(2)}, u32[]{:S(2)}) %collective-permute-start.29) | collective-permute-done | bytes 589856 | tf_op jit(solution)/shard_map/ppermute | solution.py:186
  103.2 9.1 %collective-permute-done.56.refs_21_ = bf16[4,96,768]{2,1,0:T(8,128)(2,1)} collective-permute-done((bf16[4,96,768]{2,1,0:T(8,128)(2,1)}, bf16[4,96,768]{2,1,0:T(8,128)(2,1)}, u32[]{:S(2)}, u32[]{:S(2)}) %collective-permute-start.56) | collective-permute-done | bytes 589856 | tf_op jit(solution)/shard_map/ppermute | solution.py:186
  118.2 6.7 %collective-permute-done.44.refs_11_ = bf16[4,96,768]{2,1,0:T(8,128)(2,1)} collective-permute-done((bf16[4,96,768]{2,1,0:T(8,128)(2,1)S(1)}, bf16[4,96,768]{2,1,0:T(8,128)(2,1)}, u32[]{:S(2)}, u32[]{:S(2)}) %collective-permute-start.44) | collective-permute-done | bytes 589856 | tf_op jit(solution)/shard_map/ppermute | solution.py:186
  135.4 3.9 collective-permute-done.30.refs_16_.refs_10_
  141.6 4.2 collective-permute-done.57.refs_22_
  147.4 3.4 collective-permute-done.45.refs_12_
  162.4 7.4 %space_forward.1 = (bf16[4,256,576]{2,1,0:T(8,128)(2,1)}, bf16[4,256,192]{2,1,0:T(8,128)(2,1)S(1)}, bf16[4,16,768]{2,1,0:T(8,128)(2,1)S(1)}, bf16[4,16,768]{2,1,...) custom-call(bf16[64,768]{1,0:T(8,128)(2,1)S(1)} %bitcast.328, ...), custom_call_target="tpu_custom_call" | custom-call | flops 2415919104 | bytes 7100416 | tf_op jit(solution)/shard_map/space_forward/pallas_call | solution.py:468
  170.6 5.7 %collective-permute-start.19 = (bf16[4,16,768]{2,1,0:T(8,128)(2,1)S(1)}, bf16[4,16,768]{2,1,0:T(8,128)(2,1)S(1)}, u32[]{:S(2)}, u32[]{:S(2)}) collective-permute-start(bf16[4,16,768]{2,1,0:T(8,128)(2,1)S(1)} %get-tuple-element.62), channel_id=1, source_target_pairs={{0,3},{1,0},{2,1},{3,2},{4,7},{5,4},{6,5},{7,6},{8,11},{9,8},{10,9... | collective-permute-start | bytes 294920 | tf_op jit(solution)/shard_map/ppermute | solution.py:198
  176.4 3.0 collective-permute-done.19.refs_1_
  179.7 4.1 collective-permute-done.20.refs_2_
  183.8 2.8 collective-permute-done.21.refs_3_
  209.0 7.6 %time_forward.1 = (bf16[4,256,576]{2,1,0:T(8,128)(2,1)}, bf16[4,256,192]{2,1,0:T(8,128)(2,1)S(1)}, f32[256,768]{1,0:T(8,128)}, f32[256,768]{1,0:T(8,128)}) custom-call(bf16[4,16,768]{2,1,0:T(8,128)(2,1)S(1)} %copy-done.8, bf16[4,16,768]{2,1,0:T(8,128)(2,1)S(1)} %copy-done.57, bf16[4,16,768]{2,1,0:T(8,128)(2,1)S(1)} %copy-done.61, ...), custom_call_target="tpu_custom_call" | custom-call | flops 2415919104 | bytes 8673280 | tf_op jit(solution)/shard_map/time_forward/pallas_call | solution.py:468
  216.8 16.2 %mlp.1 = (bf16[2,2,4,96,768]{4,3,2,1,0:T(8,128)(2,1)}, bf16[2,2,4,96,768]{4,3,2,1,0:T(8,128)(2,1)}, bf16[2,2,4,96,768]{4,3,2,1,0:T(8,128)(2,1)}, bf16[2,2,4,96,7...) custom-call(f32[256,768]{1,0:T(8,128)} %get-tuple-element.69.refs_0_, ...), custom_call_target="tpu_custom_call" | custom-call | flops 7247757312 | bytes 21276672 | tf_op jit(solution)/shard_map/mlp/pallas_call | solution.py:468
  233.3 17.0 %time_backward.1 = (bf16[2,2,4,96,768]{4,3,2,1,0:T(8,128)(2,1)}, bf16[2,2,4,96,768]{4,3,2,1,0:T(8,128)(2,1)}, f32[3,768]{1,0:T(4,128)S(1)}, f32[4,576]{1,0:T(4,1...) custom-call(f32[256,768]{1,0:T(8,128)} %get-tuple-element.75.refs_0_, ...), custom_call_target="tpu_custom_call" | custom-call | flops 3623878656 | bytes 13001728 | tf_op jit(solution)/shard_map/time_backward/pallas_call | solution.py:468
  252.3 4.0 collective-permute-done.68.refs_2_
  257.8 2.6 collective-permute-start.71
  262.0 3.3 collective-permute-done.70.refs_5_
  278.1 16.8 %space_backward.1 = (bf16[2,2,4,96,768]{4,3,2,1,0:T(8,128)(2,1)}, bf16[2,2,4,96,768]{4,3,2,1,0:T(8,128)(2,1)}, f32[3,768]{1,0:T(4,128)S(1)}, f32[4,576]{1,0:T(4,...) custom-call(bf16[64,768]{1,0:T(8,128)(2,1)S(1)} %bitcast.329, ...), custom_call_target="tpu_custom_call" | custom-call | flops 3623878656 | bytes 12608512 | tf_op jit(solution)/shard_map/space_backward/pallas_call | solution.py:468
  298.7 3.7 collective-permute-done.65.refs_2_
  303.2 2.8 collective-permute-start.73
  308.8 3.2 collective-permute-done.78
  312.6 11.8 %collective-permute-done.74.refs_2_ = f32[4,16,768]{2,1,0:T(8,128)S(1)} collective-permute-done((f32[4,16,768]{2,1,0:T(8,128)S(1)}, f32[4,16,768]{2,1,0:T(8,128)S(1)}, u32[]{:S(2)}, u32[]{:S(2)}) %collective-permute-start.74) | collective-permute-done | bytes 196640 | tf_op jit(solution)/shard_map/ppermute | solution.py:198
  324.4 4.3 collective-permute-done.79
  329.1 8.2 %collective-permute-done.75.refs_3_ = f32[4,16,768]{2,1,0:T(8,128)S(1)} collective-permute-done((f32[4,16,768]{2,1,0:T(8,128)S(1)}, f32[4,16,768]{2,1,0:T(8,128)S(1)}, u32[]{:S(2)}, u32[]{:S(2)}) %collective-permute-start.75) | collective-permute-done | bytes 196640 | tf_op jit(solution)/shard_map/ppermute | solution.py:198
  339.4 3.1 collective-permute-done.80
  366.7 8.9 %collective-permute-done.98 = bf16[2,2,96,768]{3,2,1,0:T(8,128)(2,1)S(1)} collective-permute-done((bf16[2,2,96,768]{3,2,1,0:T(8,128)(2,1)S(1)}, bf16[2,2,96,768]{3,2,1,0:T(8,128)(2,1)S(1)}, u32[]{:S(2)}, u32[]{:S(2)}) %collective-permute-start.98) | collective-permute-done | bytes 589856 | tf_op jit(solution)/shard_map/ppermute | solution.py:182
  379.5 8.7 %collective-permute-done.90 = bf16[2,2,96,768]{3,2,1,0:T(8,128)(2,1)S(1)} collective-permute-done((bf16[2,2,96,768]{3,2,1,0:T(8,128)(2,1)S(1)}, bf16[2,2,96,768]{3,2,1,0:T(8,128)(2,1)S(1)}, u32[]{:S(2)}, u32[]{:S(2)}) %collective-permute-start.90) | collective-permute-done | bytes 589856 | tf_op jit(solution)/shard_map/ppermute | solution.py:182
  392.1 8.7 %collective-permute-done.82 = bf16[2,2,96,768]{3,2,1,0:T(8,128)(2,1)S(1)} collective-permute-done((bf16[2,2,96,768]{3,2,1,0:T(8,128)(2,1)S(1)}, bf16[2,2,96,768]{3,2,1,0:T(8,128)(2,1)S(1)}, u32[]{:S(2)}, u32[]{:S(2)}) %collective-permute-start.82) | collective-permute-done | bytes 589856 | tf_op jit(solution)/shard_map/ppermute | solution.py:182
  408.7 4.8 %collective-permute-done.102 = bf16[2,96,768]{2,1,0:T(8,128)(2,1)S(1)} collective-permute-done((bf16[2,96,768]{2,1,0:T(8,128)(2,1)S(1)}, bf16[2,96,768]{2,1,0:T(8,128)(2,1)S(1)}, u32[]{:S(2)}, u32[]{:S(2)}) %collective-permute-start.102) | collective-permute-done | bytes 294944 | tf_op jit(solution)/shard_map/ppermute | solution.py:182
  421.5 3.8 collective-permute-done.108
  425.9 4.0 collective-permute-done.111
  429.9 4.7 collective-permute-start.96
  435.4 3.7 collective-permute-start.100
  441.0 3.2 collective-permute-done.96
  448.7 6.1 %collective-permute-start.84 = (bf16[96,768]{1,0:T(8,128)(2,1)S(1)}, bf16[96,768]{1,0:T(8,128)(2,1)S(1)}, u32[]{:S(2)}, u32[]{:S(2)}) collective-permute-start(bf16[96,768]{1,0:T(8,128)(2,1)S(1)} %fusion.45), channel_id=1, source_target_pairs={{0,1},{1,2},{2,3},{3,0},{4,5},{5,6},{6,7},{7,4},{8,9},{9,10},{10,1... | collective-permute-start | bytes 442376 | tf_op jit(solution)/shard_map/ppermute | solution.py:198
  457.7 2.9 collective-permute-start.88
  (551 shorter events, 185.7 us)
Async XLA Ops:
  8.3 16.9 %collective-permute-start.9 = (bf16[96,768]{1,0:T(8,128)(2,1)S(1)}, bf16[96,768]{1,0:T(8,128)(2,1)S(1)}, u32[]{:S(2)}, u32[]{:S(2)}) collective-permute-start(bf16[96,768]{1,0:T(8,128)(2,1)S(1)} %fusion.54), channel_id=1, source_target_pairs={{0,3},{1,0},{2,1},{3,2},{4,7},{5,4},{6,5},{7,6},{8,11},{9,8},{10,9... | collective-permute-start | bytes 442376 | tf_op jit(solution)/shard_map/ppermute | solution.py:198
  28.6 58.1 %collective-permute-start.11 = (bf16[4,96,768]{2,1,0:T(8,128)(2,1)S(1)}, bf16[4,96,768]{2,1,0:T(8,128)(2,1)}, u32[]{:S(2)}, u32[]{:S(2)}) collective-permute-start(bf16[4,96,768]{2,1,0:T(8,128)(2,1)S(1)} %pad_maximum_fusion.refs_9_.refs_13_), channel_id=1, source_target_pairs={{0,8},{4,12},{8,0},{12,4},{1,9},{5,13},{9,1},{13,5},{2,10},{6,14},... | collective-permute-start | bytes 1769480 | tf_op jit(solution)/shard_map/ppermute | solution.py:186
  30.9 16.9 %collective-permute-start.38 = (bf16[4,16,768]{2,1,0:T(8,128)(2,1)}, bf16[4,16,768]{2,1,0:T(8,128)(2,1)S(1)}, u32[]{:S(2)}, u32[]{:S(2)}) collective-permute-start(bf16[4,16,768]{2,1,0:T(8,128)(2,1)} %get-tuple-element.164), channel_id=1, source_target_pairs={{0,8},{4,12},{8,0},{12,4},{1,9},{5,13},{9,1},{13,5},{2,10},{6,14},... | collective-permute-start | bytes 294920 | tf_op jit(solution)/shard_map/ppermute | solution.py:186
  32.3 18.9 %collective-permute-start.39 = (bf16[4,16,768]{2,1,0:T(8,128)(2,1)}, bf16[4,16,768]{2,1,0:T(8,128)(2,1)S(1)}, u32[]{:S(2)}, u32[]{:S(2)}) collective-permute-start(bf16[4,16,768]{2,1,0:T(8,128)(2,1)} %get-tuple-element.163), channel_id=1, source_target_pairs={{0,12},{4,8},{8,4},{12,0},{1,13},{5,9},{9,5},{13,1},{2,14},{6,10},... | collective-permute-start | bytes 294920 | tf_op jit(solution)/shard_map/ppermute | solution.py:186
  32.8 55.7 %collective-permute-start.10 = (bf16[4,96,768]{2,1,0:T(8,128)(2,1)S(1)}, bf16[4,96,768]{2,1,0:T(8,128)(2,1)S(1)}, u32[]{:S(2)}, u32[]{:S(2)}) collective-permute-start(bf16[4,96,768]{2,1,0:T(8,128)(2,1)S(1)} %pad_maximum_fusion.refs_9_.refs_13_), channel_id=1, source_target_pairs={{0,16},{16,0},{1,17},{17,1},{2,18},{18,2},{3,19},{19,3},{4,20},{20... | collective-permute-start | bytes 1769480 | tf_op jit(solution)/shard_map/ppermute | solution.py:182
  34.4 19.6 %collective-permute-start.25 = (bf16[96,768]{1,0:T(8,128)(2,1)S(1)}, bf16[96,768]{1,0:T(8,128)(2,1)S(1)}, u32[]{:S(2)}, u32[]{:S(2)}) collective-permute-start(bf16[96,768]{1,0:T(8,128)(2,1)S(1)} %fusion.51), channel_id=1, source_target_pairs={{0,1},{1,2},{2,3},{3,0},{4,5},{5,6},{6,7},{7,4},{8,9},{9,10},{10,1... | collective-permute-start | bytes 442376 | tf_op jit(solution)/shard_map/ppermute | solution.py:198
  83.4 16.2 %collective-permute-start.29 = (bf16[4,96,768]{2,1,0:T(8,128)(2,1)S(1)}, bf16[4,96,768]{2,1,0:T(8,128)(2,1)S(1)}, u32[]{:S(2)}, u32[]{:S(2)}) collective-permute-start(bf16[4,96,768]{2,1,0:T(8,128)(2,1)S(1)} %pad_maximum_fusion.1.refs_13_.refs_7_), channel_id=1, source_target_pairs={{0,8},{4,12},{8,0},{12,4},{1,9},{5,13},{9,1},{13,5},{2,10},{6,14},... | collective-permute-start | bytes 1769480 | tf_op jit(solution)/shard_map/ppermute | solution.py:186
  85.2 16.2 %collective-permute-start.28 = (bf16[4,96,768]{2,1,0:T(8,128)(2,1)S(1)}, bf16[4,96,768]{2,1,0:T(8,128)(2,1)S(1)}, u32[]{:S(2)}, u32[]{:S(2)}) collective-permute-start(bf16[4,96,768]{2,1,0:T(8,128)(2,1)S(1)} %pad_maximum_fusion.1.refs_13_.refs_7_), channel_id=1, source_target_pairs={{0,16},{16,0},{1,17},{17,1},{2,18},{18,2},{3,19},{19,3},{4,20},{20... | collective-permute-start | bytes 1769480 | tf_op jit(solution)/shard_map/ppermute | solution.py:182
  88.5 23.8 %collective-permute-start.56 = (bf16[4,96,768]{2,1,0:T(8,128)(2,1)}, bf16[4,96,768]{2,1,0:T(8,128)(2,1)}, u32[]{:S(2)}, u32[]{:S(2)}) collective-permute-start(bf16[4,96,768]{2,1,0:T(8,128)(2,1)} %pad_maximum_fusion.3.refs_19_), channel_id=1, source_target_pairs={{0,8},{4,12},{8,0},{12,4},{1,9},{5,13},{9,1},{13,5},{2,10},{6,14},... | collective-permute-start | bytes 1769480 | tf_op jit(solution)/shard_map/ppermute | solution.py:186
  88.9 26.0 %collective-permute-start.55 = (bf16[4,96,768]{2,1,0:T(8,128)(2,1)}, bf16[4,96,768]{2,1,0:T(8,128)(2,1)}, u32[]{:S(2)}, u32[]{:S(2)}) collective-permute-start(bf16[4,96,768]{2,1,0:T(8,128)(2,1)} %pad_maximum_fusion.3.refs_19_), channel_id=1, source_target_pairs={{0,16},{16,0},{1,17},{17,1},{2,18},{18,2},{3,19},{19,3},{4,20},{20... | collective-permute-start | bytes 1769480 | tf_op jit(solution)/shard_map/ppermute | solution.py:182
  99.6 16.9 %collective-permute-start.59 = (bf16[4,96,768]{2,1,0:T(8,128)(2,1)}, bf16[4,96,768]{2,1,0:T(8,128)(2,1)}, u32[]{:S(2)}, u32[]{:S(2)}) collective-permute-start(bf16[4,96,768]{2,1,0:T(8,128)(2,1)} %pad_maximum_fusion.3.refs_19_), channel_id=1, source_target_pairs={{0,4},{4,0},{8,12},{12,8},{1,5},{5,1},{9,13},{13,9},{2,6},{6,2},{1... | collective-permute-start | bytes 1769480 | tf_op jit(solution)/shard_map/ppermute | solution.py:186
  101.4 23.5 %collective-permute-start.44 = (bf16[4,96,768]{2,1,0:T(8,128)(2,1)S(1)}, bf16[4,96,768]{2,1,0:T(8,128)(2,1)}, u32[]{:S(2)}, u32[]{:S(2)}) collective-permute-start(bf16[4,96,768]{2,1,0:T(8,128)(2,1)S(1)} %pad_maximum_fusion.2.refs_9_), channel_id=1, source_target_pairs={{0,8},{4,12},{8,0},{12,4},{1,9},{5,13},{9,1},{13,5},{2,10},{6,14},... | collective-permute-start | bytes 1769480 | tf_op jit(solution)/shard_map/ppermute | solution.py:186
  101.7 25.1 %collective-permute-start.43 = (bf16[4,96,768]{2,1,0:T(8,128)(2,1)S(1)}, bf16[4,96,768]{2,1,0:T(8,128)(2,1)}, u32[]{:S(2)}, u32[]{:S(2)}) collective-permute-start(bf16[4,96,768]{2,1,0:T(8,128)(2,1)S(1)} %pad_maximum_fusion.2.refs_9_), channel_id=1, source_target_pairs={{0,16},{16,0},{1,17},{17,1},{2,18},{18,2},{3,19},{19,3},{4,20},{20... | collective-permute-start | bytes 1769480 | tf_op jit(solution)/shard_map/ppermute | solution.py:182
  112.3 16.9 %collective-permute-start.47 = (bf16[4,96,768]{2,1,0:T(8,128)(2,1)S(1)}, bf16[4,96,768]{2,1,0:T(8,128)(2,1)}, u32[]{:S(2)}, u32[]{:S(2)}) collective-permute-start(bf16[4,96,768]{2,1,0:T(8,128)(2,1)S(1)} %pad_maximum_fusion.2.refs_9_), channel_id=1, source_target_pairs={{0,4},{4,0},{8,12},{12,8},{1,5},{5,1},{9,13},{13,9},{2,6},{6,2},{1... | collective-permute-start | bytes 1769480 | tf_op jit(solution)/shard_map/ppermute | solution.py:186
  115.0 18.3 %collective-permute-start.12 = (bf16[2,96,768]{2,1,0:T(8,128)(2,1)S(1)}, bf16[2,96,768]{2,1,0:T(8,128)(2,1)S(1)}, u32[]{:S(2)}, u32[]{:S(2)}) collective-permute-start(bf16[2,96,768]{2,1,0:T(8,128)(2,1)S(1)} %slice.664), channel_id=1, source_target_pairs={{0,16},{16,0},{1,17},{17,1},{2,18},{18,2},{3,19},{19,3},{4,20},{20... | collective-permute-start | bytes 884744 | tf_op jit(solution)/shard_map/ppermute | solution.py:182
  116.5 18.4 %collective-permute-start.13 = (bf16[2,96,768]{2,1,0:T(8,128)(2,1)S(1)}, bf16[2,96,768]{2,1,0:T(8,128)(2,1)S(1)}, u32[]{:S(2)}, u32[]{:S(2)}) collective-permute-start(bf16[2,96,768]{2,1,0:T(8,128)(2,1)S(1)} %slice.665), channel_id=1, source_target_pairs={{0,8},{4,12},{8,0},{12,4},{1,9},{5,13},{9,1},{13,5},{2,10},{6,14},... | collective-permute-start | bytes 884744 | tf_op jit(solution)/shard_map/ppermute | solution.py:186
  129.2 16.6 %collective-permute-start.57 = (bf16[2,96,768]{2,1,0:T(8,128)(2,1)S(1)}, bf16[2,96,768]{2,1,0:T(8,128)(2,1)}, u32[]{:S(2)}, u32[]{:S(2)}) collective-permute-start(bf16[2,96,768]{2,1,0:T(8,128)(2,1)S(1)} %slice.680), channel_id=1, source_target_pairs={{0,16},{16,0},{1,17},{17,1},{2,18},{18,2},{3,19},{19,3},{4,20},{20... | collective-permute-start | bytes 884744 | tf_op jit(solution)/shard_map/ppermute | solution.py:182
  152.8 17.8 %collective-permute-start.33 = (bf16[4,96,768]{2,1,0:T(8,128)(2,1)S(1)}, bf16[4,96,768]{2,1,0:T(8,128)(2,1)S(1)}, u32[]{:S(2)}, u32[]{:S(2)}) collective-permute-start(bf16[4,96,768]{2,1,0:T(8,128)(2,1)S(1)} %collective-permute-done.28.refs_14_.refs_8_), channel_id=1, source_target_pairs={{0,4},{4,0},{8,12},{12,8},{1,5},{5,1},{9,13},{13,9},{2,6},{6,2},{1... | collective-permute-start | bytes 1769480 | tf_op jit(solution)/shard_map/ppermute | solution.py:186
  152.8 23.4 %collective-permute-start.34 = (bf16[4,96,768]{2,1,0:T(8,128)(2,1)S(1)}, bf16[4,96,768]{2,1,0:T(8,128)(2,1)S(1)}, u32[]{:S(2)}, u32[]{:S(2)}) collective-permute-start(bf16[4,96,768]{2,1,0:T(8,128)(2,1)S(1)} %collective-permute-done.29.refs_15_.refs_9_), channel_id=1, source_target_pairs={{0,4},{4,0},{8,12},{12,8},{1,5},{5,1},{9,13},{13,9},{2,6},{6,2},{1... | collective-permute-start | bytes 1769480 | tf_op jit(solution)/shard_map/ppermute | solution.py:186
  153.3 22.9 %collective-permute-start.60 = (bf16[4,96,768]{2,1,0:T(8,128)(2,1)}, bf16[4,96,768]{2,1,0:T(8,128)(2,1)S(1)}, u32[]{:S(2)}, u32[]{:S(2)}) collective-permute-start(bf16[4,96,768]{2,1,0:T(8,128)(2,1)} %collective-permute-done.55.refs_20_), channel_id=1, source_target_pairs={{0,4},{4,0},{8,12},{12,8},{1,5},{5,1},{9,13},{13,9},{2,6},{6,2},{1... | collective-permute-start | bytes 1769480 | tf_op jit(solution)/shard_map/ppermute | solution.py:186
  154.1 33.1 %collective-permute-start.61 = (bf16[4,96,768]{2,1,0:T(8,128)(2,1)}, bf16[4,96,768]{2,1,0:T(8,128)(2,1)S(1)}, u32[]{:S(2)}, u32[]{:S(2)}) collective-permute-start(bf16[4,96,768]{2,1,0:T(8,128)(2,1)} %collective-permute-done.56.refs_21_), channel_id=1, source_target_pairs={{0,4},{4,0},{8,12},{12,8},{1,5},{5,1},{9,13},{13,9},{2,6},{6,2},{1... | collective-permute-start | bytes 1769480 | tf_op jit(solution)/shard_map/ppermute | solution.py:186
  154.6 33.1 %collective-permute-start.48 = (bf16[4,96,768]{2,1,0:T(8,128)(2,1)}, bf16[4,96,768]{2,1,0:T(8,128)(2,1)S(1)}, u32[]{:S(2)}, u32[]{:S(2)}) collective-permute-start(bf16[4,96,768]{2,1,0:T(8,128)(2,1)} %collective-permute-done.43.refs_10_), channel_id=1, source_target_pairs={{0,4},{4,0},{8,12},{12,8},{1,5},{5,1},{9,13},{13,9},{2,6},{6,2},{1... | collective-permute-start | bytes 1769480 | tf_op jit(solution)/shard_map/ppermute | solution.py:186
  186.6 30.0 %collective-permute-start.49 = (bf16[4,96,768]{2,1,0:T(8,128)(2,1)}, bf16[4,96,768]{2,1,0:T(8,128)(2,1)}, u32[]{:S(2)}, u32[]{:S(2)}) collective-permute-start(bf16[4,96,768]{2,1,0:T(8,128)(2,1)} %collective-permute-done.44.refs_11_), channel_id=1, source_target_pairs={{0,4},{4,0},{8,12},{12,8},{1,5},{5,1},{9,13},{13,9},{2,6},{6,2},{1... | collective-permute-start | bytes 1769480 | tf_op jit(solution)/shard_map/ppermute | solution.py:186
  190.6 25.9 %collective-permute-start.62 = (bf16[2,96,768]{2,1,0:T(8,128)(2,1)}, bf16[2,96,768]{2,1,0:T(8,128)(2,1)}, u32[]{:S(2)}, u32[]{:S(2)}) collective-permute-start(bf16[2,96,768]{2,1,0:T(8,128)(2,1)} %collective-permute-done.57.refs_22_), channel_id=1, source_target_pairs={{0,4},{4,0},{8,12},{12,8},{1,5},{5,1},{9,13},{13,9},{2,6},{6,2},{1... | collective-permute-start | bytes 884744 | tf_op jit(solution)/shard_map/ppermute | solution.py:186
  192.0 24.6 %collective-permute-start.63 = (bf16[2,96,768]{2,1,0:T(8,128)(2,1)}, bf16[2,96,768]{2,1,0:T(8,128)(2,1)}, u32[]{:S(2)}, u32[]{:S(2)}) collective-permute-start(bf16[2,96,768]{2,1,0:T(8,128)(2,1)} %collective-permute-done.58.refs_23_), channel_id=1, source_target_pairs={{0,4},{4,0},{8,12},{12,8},{1,5},{5,1},{9,13},{13,9},{2,6},{6,2},{1... | collective-permute-start | bytes 884744 | tf_op jit(solution)/shard_map/ppermute | solution.py:186
  193.9 22.7 %collective-permute-start.50 = (bf16[2,96,768]{2,1,0:T(8,128)(2,1)}, bf16[2,96,768]{2,1,0:T(8,128)(2,1)}, u32[]{:S(2)}, u32[]{:S(2)}) collective-permute-start(bf16[2,96,768]{2,1,0:T(8,128)(2,1)} %collective-permute-done.45.refs_12_), channel_id=1, source_target_pairs={{0,4},{4,0},{8,12},{12,8},{1,5},{5,1},{9,13},{13,9},{2,6},{6,2},{1... | collective-permute-start | bytes 884744 | tf_op jit(solution)/shard_map/ppermute | solution.py:186
  194.6 22.0 %collective-permute-start.51 = (bf16[2,96,768]{2,1,0:T(8,128)(2,1)}, bf16[2,96,768]{2,1,0:T(8,128)(2,1)}, u32[]{:S(2)}, u32[]{:S(2)}) collective-permute-start(bf16[2,96,768]{2,1,0:T(8,128)(2,1)} %collective-permute-done.46.refs_13_), channel_id=1, source_target_pairs={{0,4},{4,0},{8,12},{12,8},{1,5},{5,1},{9,13},{13,9},{2,6},{6,2},{1... | collective-permute-start | bytes 884744 | tf_op jit(solution)/shard_map/ppermute | solution.py:186
  233.1 111.5 %collective-permute-start.105 = (bf16[2,2,4,96,768]{4,3,2,1,0:T(8,128)(2,1)}, bf16[2,2,4,96,768]{4,3,2,1,0:T(8,128)(2,1)}, u32[]{:S(2)}, u32[]{:S(2)}) collective-permute-start(bf16[2,2,4,96,768]{4,3,2,1,0:T(8,128)(2,1)} %get-tuple-element.106), channel_id=1, source_target_pairs={{0,4},{4,0},{8,12},{12,8},{1,5},{5,1},{9,13},{13,9},{2,6},{6,2},{1... | collective-permute-start | bytes 7077896 | tf_op jit(solution)/shard_map/ppermute | solution.py:186
  261.9 88.6 %collective-permute-start.97 = (bf16[2,2,4,96,768]{4,3,2,1,0:T(8,128)(2,1)}, bf16[2,2,4,96,768]{4,3,2,1,0:T(8,128)(2,1)}, u32[]{:S(2)}, u32[]{:S(2)}) collective-permute-start(bf16[2,2,4,96,768]{4,3,2,1,0:T(8,128)(2,1)} %get-tuple-element.104), channel_id=1, source_target_pairs={{0,4},{4,0},{8,12},{12,8},{1,5},{5,1},{9,13},{13,9},{2,6},{6,2},{1... | collective-permute-start | bytes 7077896 | tf_op jit(solution)/shard_map/ppermute | solution.py:186
  265.9 88.5 %collective-permute-start.89 = (bf16[2,2,4,96,768]{4,3,2,1,0:T(8,128)(2,1)}, bf16[2,2,4,96,768]{4,3,2,1,0:T(8,128)(2,1)}, u32[]{:S(2)}, u32[]{:S(2)}) collective-permute-start(bf16[2,2,4,96,768]{4,3,2,1,0:T(8,128)(2,1)} %get-tuple-element.102), channel_id=1, source_target_pairs={{0,4},{4,0},{8,12},{12,8},{1,5},{5,1},{9,13},{13,9},{2,6},{6,2},{1... | collective-permute-start | bytes 7077896 | tf_op jit(solution)/shard_map/ppermute | solution.py:186
  312.0 47.0 %collective-permute-start.81 = (bf16[2,2,4,96,768]{4,3,2,1,0:T(8,128)(2,1)}, bf16[2,2,4,96,768]{4,3,2,1,0:T(8,128)(2,1)}, u32[]{:S(2)}, u32[]{:S(2)}) collective-permute-start(bf16[2,2,4,96,768]{4,3,2,1,0:T(8,128)(2,1)} %get-tuple-element.100), channel_id=1, source_target_pairs={{0,4},{4,0},{8,12},{12,8},{1,5},{5,1},{9,13},{13,9},{2,6},{6,2},{1... | collective-permute-start | bytes 7077896 | tf_op jit(solution)/shard_map/ppermute | solution.py:186
  346.6 16.9 %collective-permute-start.106 = (bf16[2,2,96,768]{3,2,1,0:T(8,128)(2,1)S(1)}, bf16[2,2,96,768]{3,2,1,0:T(8,128)(2,1)S(1)}, u32[]{:S(2)}, u32[]{:S(2)}) collective-permute-start(bf16[2,2,96,768]{3,2,1,0:T(8,128)(2,1)S(1)} %get-tuple-element.134), channel_id=1, source_target_pairs={{0,16},{16,0},{1,17},{17,1},{2,18},{18,2},{3,19},{19,3},{4,20},{20... | collective-permute-start | bytes 1769480 | tf_op jit(solution)/shard_map/ppermute | solution.py:182
  349.6 16.3 %collective-permute-start.109 = (bf16[2,2,96,768]{3,2,1,0:T(8,128)(2,1)S(1)}, bf16[2,2,96,768]{3,2,1,0:T(8,128)(2,1)S(1)}, u32[]{:S(2)}, u32[]{:S(2)}) collective-permute-start(bf16[2,2,96,768]{3,2,1,0:T(8,128)(2,1)S(1)} %get-tuple-element.136), channel_id=1, source_target_pairs={{0,8},{4,12},{8,0},{12,4},{1,9},{5,13},{9,1},{13,5},{2,10},{6,14},... | collective-permute-start | bytes 1769480 | tf_op jit(solution)/shard_map/ppermute | solution.py:186
  352.1 23.5 %collective-permute-start.98 = (bf16[2,2,96,768]{3,2,1,0:T(8,128)(2,1)S(1)}, bf16[2,2,96,768]{3,2,1,0:T(8,128)(2,1)S(1)}, u32[]{:S(2)}, u32[]{:S(2)}) collective-permute-start(bf16[2,2,96,768]{3,2,1,0:T(8,128)(2,1)S(1)} %get-tuple-element.138), channel_id=1, source_target_pairs={{0,16},{16,0},{1,17},{17,1},{2,18},{18,2},{3,19},{19,3},{4,20},{20... | collective-permute-start | bytes 1769480 | tf_op jit(solution)/shard_map/ppermute | solution.py:182
  354.4 24.3 %collective-permute-start.101 = (bf16[2,2,96,768]{3,2,1,0:T(8,128)(2,1)S(1)}, bf16[2,2,96,768]{3,2,1,0:T(8,128)(2,1)S(1)}, u32[]{:S(2)}, u32[]{:S(2)}) collective-permute-start(bf16[2,2,96,768]{3,2,1,0:T(8,128)(2,1)S(1)} %get-tuple-element.140), channel_id=1, source_target_pairs={{0,8},{4,12},{8,0},{12,4},{1,9},{5,13},{9,1},{13,5},{2,10},{6,14},... | collective-permute-start | bytes 1769480 | tf_op jit(solution)/shard_map/ppermute | solution.py:186
  359.0 29.2 %collective-permute-start.90 = (bf16[2,2,96,768]{3,2,1,0:T(8,128)(2,1)S(1)}, bf16[2,2,96,768]{3,2,1,0:T(8,128)(2,1)S(1)}, u32[]{:S(2)}, u32[]{:S(2)}) collective-permute-start(bf16[2,2,96,768]{3,2,1,0:T(8,128)(2,1)S(1)} %get-tuple-element.142), channel_id=1, source_target_pairs={{0,16},{16,0},{1,17},{17,1},{2,18},{18,2},{3,19},{19,3},{4,20},{20... | collective-permute-start | bytes 1769480 | tf_op jit(solution)/shard_map/ppermute | solution.py:182
  363.5 27.7 %collective-permute-start.93 = (bf16[2,2,96,768]{3,2,1,0:T(8,128)(2,1)S(1)}, bf16[2,2,96,768]{3,2,1,0:T(8,128)(2,1)S(1)}, u32[]{:S(2)}, u32[]{:S(2)}) collective-permute-start(bf16[2,2,96,768]{3,2,1,0:T(8,128)(2,1)S(1)} %get-tuple-element.144), channel_id=1, source_target_pairs={{0,8},{4,12},{8,0},{12,4},{1,9},{5,13},{9,1},{13,5},{2,10},{6,14},... | collective-permute-start | bytes 1769480 | tf_op jit(solution)/shard_map/ppermute | solution.py:186
  366.0 34.8 %collective-permute-start.82 = (bf16[2,2,96,768]{3,2,1,0:T(8,128)(2,1)S(1)}, bf16[2,2,96,768]{3,2,1,0:T(8,128)(2,1)S(1)}, u32[]{:S(2)}, u32[]{:S(2)}) collective-permute-start(bf16[2,2,96,768]{3,2,1,0:T(8,128)(2,1)S(1)} %get-tuple-element.146), channel_id=1, source_target_pairs={{0,16},{16,0},{1,17},{17,1},{2,18},{18,2},{3,19},{19,3},{4,20},{20... | collective-permute-start | bytes 1769480 | tf_op jit(solution)/shard_map/ppermute | solution.py:182
  375.6 28.3 %collective-permute-start.85 = (bf16[2,2,96,768]{3,2,1,0:T(8,128)(2,1)S(1)}, bf16[2,2,96,768]{3,2,1,0:T(8,128)(2,1)S(1)}, u32[]{:S(2)}, u32[]{:S(2)}) collective-permute-start(bf16[2,2,96,768]{3,2,1,0:T(8,128)(2,1)S(1)} %get-tuple-element.148), channel_id=1, source_target_pairs={{0,8},{4,12},{8,0},{12,4},{1,9},{5,13},{9,1},{13,5},{2,10},{6,14},... | collective-permute-start | bytes 1769480 | tf_op jit(solution)/shard_map/ppermute | solution.py:186
  378.6 36.4 %collective-permute-start.107 = (bf16[2,96,768]{2,1,0:T(8,128)(2,1)S(1)}, bf16[2,96,768]{2,1,0:T(8,128)(2,1)S(1)}, u32[]{:S(2)}, u32[]{:S(2)}) collective-permute-start(bf16[2,96,768]{2,1,0:T(8,128)(2,1)S(1)} %fusion.22), channel_id=1, source_target_pairs={{0,8},{4,12},{8,0},{12,4},{1,9},{5,13},{9,1},{13,5},{2,10},{6,14},... | collective-permute-start | bytes 884744 | tf_op jit(solution)/shard_map/ppermute | solution.py:186
  388.2 19.0 %collective-permute-start.110 = (bf16[2,96,768]{2,1,0:T(8,128)(2,1)S(1)}, bf16[2,96,768]{2,1,0:T(8,128)(2,1)S(1)}, u32[]{:S(2)}, u32[]{:S(2)}) collective-permute-start(bf16[2,96,768]{2,1,0:T(8,128)(2,1)S(1)} %fusion.23), channel_id=1, source_target_pairs={{0,16},{16,0},{1,17},{17,1},{2,18},{18,2},{3,19},{19,3},{4,20},{20... | collective-permute-start | bytes 884744 | tf_op jit(solution)/shard_map/ppermute | solution.py:182
  391.3 25.3 %collective-permute-start.99 = (bf16[2,96,768]{2,1,0:T(8,128)(2,1)S(1)}, bf16[2,96,768]{2,1,0:T(8,128)(2,1)S(1)}, u32[]{:S(2)}, u32[]{:S(2)}) collective-permute-start(bf16[2,96,768]{2,1,0:T(8,128)(2,1)S(1)} %fusion.20), channel_id=1, source_target_pairs={{0,8},{4,12},{8,0},{12,4},{1,9},{5,13},{9,1},{13,5},{2,10},{6,14},... | collective-permute-start | bytes 884744 | tf_op jit(solution)/shard_map/ppermute | solution.py:186
  403.9 16.3 %collective-permute-start.91 = (bf16[2,96,768]{2,1,0:T(8,128)(2,1)S(1)}, bf16[2,96,768]{2,1,0:T(8,128)(2,1)S(1)}, u32[]{:S(2)}, u32[]{:S(2)}) collective-permute-start(bf16[2,96,768]{2,1,0:T(8,128)(2,1)S(1)} %fusion.18), channel_id=1, source_target_pairs={{0,8},{4,12},{8,0},{12,4},{1,9},{5,13},{9,1},{13,5},{2,10},{6,14},... | collective-permute-start | bytes 884744 | tf_op jit(solution)/shard_map/ppermute | solution.py:186
  413.5 34.3 %collective-permute-start.83 = (bf16[2,96,768]{2,1,0:T(8,128)(2,1)}, bf16[2,96,768]{2,1,0:T(8,128)(2,1)}, u32[]{:S(2)}, u32[]{:S(2)}) collective-permute-start(bf16[2,96,768]{2,1,0:T(8,128)(2,1)} %fusion.16), channel_id=1, source_target_pairs={{0,8},{4,12},{8,0},{12,4},{1,9},{5,13},{9,1},{13,5},{2,10},{6,14},... | collective-permute-start | bytes 884744 | tf_op jit(solution)/shard_map/ppermute | solution.py:186
  415.1 39.8 %collective-permute-start.86 = (bf16[2,96,768]{2,1,0:T(8,128)(2,1)}, bf16[2,96,768]{2,1,0:T(8,128)(2,1)}, u32[]{:S(2)}, u32[]{:S(2)}) collective-permute-start(bf16[2,96,768]{2,1,0:T(8,128)(2,1)} %fusion.17), channel_id=1, source_target_pairs={{0,16},{16,0},{1,17},{17,1},{2,18},{18,2},{3,19},{19,3},{4,20},{20... | collective-permute-start | bytes 884744 | tf_op jit(solution)/shard_map/ppermute | solution.py:182
  435.4 22.3 %collective-permute-start.100 = (bf16[96,768]{1,0:T(8,128)(2,1)}, bf16[96,768]{1,0:T(8,128)(2,1)}, u32[]{:S(2)}, u32[]{:S(2)}) collective-permute-start(bf16[96,768]{1,0:T(8,128)(2,1)} %fusion.33), channel_id=1, source_target_pairs={{0,1},{1,2},{2,3},{3,0},{4,5},{5,6},{6,7},{7,4},{8,9},{9,10},{10,1... | collective-permute-start | bytes 442376 | tf_op jit(solution)/shard_map/ppermute | solution.py:198
  440.5 20.1 %collective-permute-start.103 = (bf16[96,768]{1,0:T(8,128)(2,1)}, bf16[96,768]{1,0:T(8,128)(2,1)}, u32[]{:S(2)}, u32[]{:S(2)}) collective-permute-start(bf16[96,768]{1,0:T(8,128)(2,1)} %get-tuple-element.151), channel_id=1, source_target_pairs={{0,2},{1,3},{2,0},{3,1},{4,6},{5,7},{6,4},{7,5},{8,10},{9,11},{10,... | collective-permute-start | bytes 442376 | tf_op jit(solution)/shard_map/ppermute | solution.py:198
  444.2 16.4 %collective-permute-start.104 = (bf16[96,768]{1,0:T(8,128)(2,1)}, bf16[96,768]{1,0:T(8,128)(2,1)}, u32[]{:S(2)}, u32[]{:S(2)}) collective-permute-start(bf16[96,768]{1,0:T(8,128)(2,1)} %get-tuple-element.152), channel_id=1, source_target_pairs={{0,3},{1,0},{2,1},{3,2},{4,7},{5,4},{6,5},{7,6},{8,11},{9,8},{10,9... | collective-permute-start | bytes 442376 | tf_op jit(solution)/shard_map/ppermute | solution.py:198
  (188 other events, 2081.8 us)
